TPU v7x, 32 devices: a whole 2x2x4 slice. The times are simulated.
32 devices in a mesh: groups: 2 (over x), chan: 16 (over z, y, core).
Axes of the slice: x: 2, y: 2, z: 4, core: 2. Of those that a mesh axis runs over, the one named last changes fastest.
Arguments:
- maps: bfloat16 [4, 3072, 256], P('groups', 'chan'), parts along dimension 0, may hold values from -6 to 6
- kernels: bfloat16 [1, 9, 3072, 3072], P(None, None, 'chan'), may hold values from -0.0546875 to 0.0546875
- bias: float32 [1, 3072], P(None, 'chan'), may hold values from -3 to 3
Outputs:
- features: bfloat16 [4, 3072, 256], P('groups', 'chan'), parts along dimension 0
There are 2 independent parts, one for each index of `groups`. A program takes and returns all parts, laid end to end along the dimension named above; an argument that names none is the same for every part. Nothing has to cross between parts.
All inputs are finite; a program needn't handle non-finite values.
Results may differ from a plain program's by a relative error of at most 0.0011.
Values may be sent and summed in bfloat16 or wider, within the bound.
No kernel may reach another device: no remote copies, remote signals or barrier semaphores. Data moves between devices by JAX's collectives and lax.ppermute only.
A program may use at most 64 MiB of HBM per device.

v0:
```python
import jax
import jax.numpy as jnp
from jax import lax
from jax.sharding import PartitionSpec as P


def make_patches(stack):
    count = stack.shape[0]
    depth = stack.shape[1]
    images = stack.reshape(count, depth, 16, 16)
    padded = jnp.pad(images, ((0, 0), (0, 0), (1, 1), (1, 1)))
    shifted = [padded[:, :, row : row + 16, col : col + 16] for row in range(3) for col in range(3)]
    joined = jnp.stack(shifted, 0)
    return jnp.transpose(joined, (0, 2, 1, 3, 4)).reshape(9 * depth, count * 256)


def finish(stack, total, layer_bias):
    count = stack.shape[0]
    owned = stack.shape[1]
    activated = jnp.maximum(total + layer_bias[:, None], 0.0)
    activated = jnp.transpose(activated.reshape(owned, count, 256), (1, 0, 2))
    return (stack.astype(jnp.float32) + activated).astype(jnp.bfloat16)


def conv_by_inputs(stack, layer_kernel, layer_bias):
    owned = stack.shape[1]
    columns = make_patches(stack)
    flat = layer_kernel.reshape(9 * owned, layer_kernel.shape[2])
    total = lax.psum_scatter(
        lax.dot_general(
            flat, columns, (((0,), (0,)), ((), ())), preferred_element_type=jnp.float32
        ),
        "chan",
        scatter_dimension=0,
        tiled=True,
    )
    return finish(stack, total, layer_bias)


def local(maps, kernels, bias):
    stacks = [maps]
    updated = []
    for stack in stacks:
        updated.append(conv_by_inputs(stack, kernels[0], bias[0]))
    return updated[0]


def solution(mesh):
    in_specs = (P("groups", "chan", None), P(None, None, "chan", None), P(None, "chan"))
    out_specs = P("groups", "chan", None)
    return jax.shard_map(local, mesh=mesh, in_specs=in_specs, out_specs=out_specs, check_vma=False)
```

profile of v0, /device:TPU:0, one launch (start us, length us, event | category | flops | bytes accessed | tf_op | source)
XLA Modules:
  0.0 131.5 jit_solution(138382344292835691)
XLA Ops:
  6.5 0.0 reduce-scatter.4.cloned.1.call-start
  6.5 1.1 copy.9
  7.6 0.1 fusion.2
  7.7 0.1 fusion.6
  7.8 0.1 fusion.8
  7.9 0.1 fusion.10
  8.0 0.1 fusion.12
  8.1 0.1 fusion.16
  8.2 4.1 %copy.11 = bf16[9,192,2,16,16]{1,0,4,3,2:T(8,128)(2,1)} copy(bf16[9,192,2,16,16]{1,4,3,2,0:T(8,128)(2,1)S(1)} %bitcast.58) | data formatting | bytes 3538944 | tf_op jit(solution)/shard_map/transpose | solution.py:14
  12.3 5.3 %reshape.12 = bf16[1728,512]{0,1:T(8,128)(2,1)S(1)} reshape(bf16[9,192,2,16,16]{1,0,4,3,2:T(8,128)(2,1)} %copy.11) | data formatting | bytes 3538944 | tf_op jit(solution)/shard_map/reshape | solution.py:14
  17.5 10.3 %convolution_bitcast_fusion = f32[3072,512]{0,1:T(8,128)} fusion(bf16[1728,512]{0,1:T(8,128)(2,1)S(1)} %reshape.12, bf16[1728,3072]{1,0:T(8,128)(2,1)} %bitcast.61), kind=kOutput, calls=%fused_computation | convolution fusion | flops 5435817984 | bytes 18677760 | tf_op jit(solution)/shard_map/dot_general | solution.py:30
  27.9 6.6 %copy.13 = f32[3072,512]{1,0:T(8,128)} copy(f32[3072,512]{0,1:T(8,128)} %convolution_bitcast_fusion) | data formatting | bytes 12582912
  34.4 0.0 copy-start.1
  34.4 0.0 reduce-scatter.4.cloned.1.call-update
  34.5 0.0 copy-start
  34.5 88.0 %reduce-scatter.4.cloned.1.call-done = f32[192,512]{1,0:T(8,128)} async-done(((f32[3072,512]{1,0:T(8,128)}), f32[192,512]{1,0:T(8,128)}) %reduce-scatter.4.cloned.1.call-update) | async-done | bytes 393232
  122.5 1.2 copy.14
  123.7 0.0 copy-done.1
  123.8 0.2 copy.12
  124.0 0.0 copy-done
  124.0 0.7 fusion
  (4 shorter events, 0.1 us)
Async XLA Ops:
  6.5 116.0 %reduce-scatter.4.cloned.1.call-start = ((), (), s32[]{:S(2)}) async-start(), calls=%async_computation.1 | async-start | bytes 6684672
  34.4 89.3 %copy-start.1 = (f32[1,192]{1,0:T(1,128)S(1)}, f32[1,192]{1,0:T(1,128)}, u32[]{:S(2)}) copy-start(f32[1,192]{1,0:T(1,128)} %param.5) | copy-start | bytes 2308
  34.5 89.5 %copy-start = (bf16[2,192,256]{2,1,0:T(8,128)(2,1)S(1)}, bf16[2,192,256]{2,1,0:T(8,128)(2,1)}, u32[]{:S(2)}) copy-start(bf16[2,192,256]{2,1,0:T(8,128)(2,1)} %param.3) | copy-start | bytes 589828
Sparse Core Ops, SparseCore 0:
  34.6 87.8 reduce-scatter.3
where the time goes:
time: 132 us
  waiting for transfers between devices  88.1 us (67%)
  local copies, waits for them, and re-layouts  18.9 us (14%)
  between operations  13.5 us (10%)
  matrix products  10.3 us (8%)
    unnamed x2, waiting for transfers between devices  88.1 us
    dot_general x1, matrix products, conv_by_inputs(): lax.dot_general(flat, columns, (((0,), (0,)), ((), ())), preferred_elemen...  10.3 us
    unnamed x15, local copies, waits for them, and re-layouts  9.3 us
    reshape x1, local copies, waits for them, and re-layouts, make_patches(): jnp.transpose(joined, (0, 2, 1, 3, 4)).reshape(9 * depth, count * 256)  5.26 us
    transpose x1, local copies, waits for them, and re-layouts, make_patches(): jnp.transpose(joined, (0, 2, 1, 3, 4)).reshape(9 * depth, count * 256)  4.06 us
  transfers between devices with their start and end apart: 1, of which 1 were waited for; matrix products, arithmetic and copies ran while one was open for 0% of the time, Pallas kernels for 0%

commit v1 on v0

v1 whole, which is shorter than its diff:
```python
import functools
import math

import jax
import jax.numpy as jnp
from jax import lax
from jax.experimental import pallas as pl
from jax.experimental.pallas import tpu as pltpu
from jax.sharding import PartitionSpec as P

AXIS = "chan"
SENT = jnp.float16


def make_patches(stack):
    count, depth, pixels = stack.shape
    side = math.isqrt(pixels)
    images = stack.reshape(count, depth, side, side)
    padded = jnp.pad(images, ((0, 0), (0, 0), (1, 1), (1, 1)))
    shifted = [padded[:, :, row : row + side, col : col + side] for row in range(3) for col in range(3)]
    joined = jnp.stack(shifted, 0)
    return jnp.transpose(joined, (0, 2, 1, 3, 4)).reshape(9 * depth, count * pixels)


def finish(stack, total, layer_bias):
    count, owned, pixels = stack.shape
    activated = jnp.maximum(total + layer_bias[:, None], 0.0)
    activated = jnp.transpose(activated.reshape(owned, count, pixels), (1, 0, 2))
    return (stack.astype(jnp.float32) + activated).astype(jnp.bfloat16)


def conv_plain(stack, flat, layer_bias):
    columns = make_patches(stack)
    total = lax.psum_scatter(
        lax.dot_general(flat, columns, (((0,), (0,)), ((), ())), preferred_element_type=jnp.float32),
        AXIS,
        scatter_dimension=0,
        tiled=True,
    )
    return finish(stack, total, layer_bias)


def write_patches(maps_ref, x_ref):
    count, depth, pixels = maps_ref.shape
    side = math.isqrt(pixels)
    lane = lax.broadcasted_iota(jnp.int32, (depth, pixels), 1)
    row, col = lane // side, lane % side
    for m in range(count):
        image = maps_ref[m]
        wide = image.astype(jnp.float32)
        for tap in range(9):
            dy, dx = tap // 3 - 1, tap % 3 - 1
            shift = dy * side + dx
            value = image
            if shift:
                value = pltpu.roll(wide, (-shift) % pixels, 1)
                for step, place in ((dy, row), (dx, col)):
                    if step > 0:
                        value = jnp.where(place < side - 1, value, 0.0)
                    elif step < 0:
                        value = jnp.where(place > 0, value, 0.0)
                value = value.astype(jnp.bfloat16)
            x_ref[tap * depth : (tap + 1) * depth, m * pixels : (m + 1) * pixels] = value


def partial_kernel(m, first, source, w_ref, *refs):
    if first:
        x_ref, send_ref, keep_ref, w_buf, sem = refs
    else:
        send_ref, keep_ref, w_buf, sem = refs
        x_ref = source
    me = lax.axis_index(AXIS)
    low, pair = lax.rem(me, 2), lax.div(me, 2)
    width = w_buf.shape[2]
    owned = width // 2
    copies = []
    for j in (1, 0):
        start = pl.multiple_of((pair ^ (2 * m + j)) * width, 128)
        copy = pltpu.make_async_copy(w_ref.at[:, pl.ds(start, width)], w_buf.at[j], sem.at[j])
        copy.start()
        copies.append((j, copy))
    if first:
        write_patches(source, x_ref)
    for j, copy in copies:
        copy.wait()
        part = lax.dot_general(
            w_buf[j], x_ref[...], (((0,), (0,)), ((), ())), preferred_element_type=jnp.float32
        )

        @pl.when(low == 0)
        def _():
            keep_ref[j] = part[:owned]
            send_ref[j] = part[owned:]

        @pl.when(low == 1)
        def _():
            keep_ref[j] = part[owned:]
            send_ref[j] = part[:owned]


def partials(m, first, source, flat, owned, columns):
    depth = flat.shape[0]
    vmem = pl.BlockSpec(memory_space=pltpu.VMEM)
    half = jax.ShapeDtypeStruct((2, owned, columns), jnp.float32)
    patches = jax.ShapeDtypeStruct((depth, columns), jnp.bfloat16)
    return pl.pallas_call(
        functools.partial(partial_kernel, m, first),
        in_specs=[vmem, pl.BlockSpec(memory_space=pltpu.HBM)],
        out_specs=[vmem] * (3 if first else 2),
        out_shape=([patches] if first else []) + [half, half],
        scratch_shapes=[pltpu.VMEM((2, depth, 2 * owned), jnp.bfloat16), pltpu.SemaphoreType.DMA((2,))],
        compiler_params=pltpu.CompilerParams(vmem_limit_bytes=32 * 2**20),
        cost_estimate=pl.CostEstimate(
            flops=2 * depth * 4 * owned * columns,
            bytes_accessed=2 * depth * 4 * owned,
            transcendentals=0,
        ),
        name=f"partials_{m}",
    )(source, flat)


def conv_halving(stack, flat, layer_bias, size):
    count, owned, pixels = stack.shape
    columns = count * pixels

    def swap(value, bit):
        return lax.ppermute(value, AXIS, [(i, i ^ bit) for i in range(size)])

    chunks = size // 4
    sums = {}
    patches = None
    for m in reversed(range(chunks)):
        if patches is None:
            patches, send, keep = partials(m, True, stack, flat, owned, columns)
        else:
            send, keep = partials(m, False, patches, flat, owned, columns)
        came = swap(send, 1)
        second = swap((keep[1] + came[1]).astype(SENT), 2)
        sums[m] = keep[0] + came[0] + second.astype(jnp.float32)
    bit = 1
    while bit < chunks:
        for m in reversed(range(chunks)):
            if m % bit == 0 and m & bit:
                came = swap(sums[m].astype(SENT), 4 * bit)
                sums[m - bit] = sums[m - bit] + came.astype(jnp.float32)
        bit *= 2
    return finish(stack, sums[0], layer_bias)


def local(size, maps, kernels, bias):
    for layer in range(kernels.shape[0]):
        owned = maps.shape[1]
        flat = kernels[layer].reshape(9 * owned, kernels.shape[3])
        if size >= 4 and size & (size - 1) == 0 and owned % 64 == 0 and maps.shape[2] % 128 == 0:
            maps = conv_halving(maps, flat, bias[layer], size)
        else:
            maps = conv_plain(maps, flat, bias[layer])
    return maps


def solution(mesh):
    in_specs = (P("groups", AXIS, None), P(None, None, AXIS, None), P(None, AXIS))
    out_specs = P("groups", AXIS, None)
    return jax.shard_map(
        functools.partial(local, mesh.shape[AXIS]), mesh=mesh, in_specs=in_specs, out_specs=out_specs, check_vma=False
    )
```

time: 132 us -> 48.3 us (0.37)
  waiting for transfers between devices: 88.1 us -> 17.8 us
  between operations: 13.5 us -> 0.09 us
  starting transfers between devices: 0.01 us -> 13.4 us
  local copies, waits for them, and re-layouts: 18.9 us -> 5.59 us
  matrix products: 10.3 us -> 0 us
  Pallas kernels: 0 us -> 9.66 us
    unnamed x2 -> x0, waiting for transfers between devices: 88.1 us -> none
    ppermute x0 -> x11, waiting for transfers between devices: none -> 17.8 us  [swap(): return lax.ppermute(value, AXIS, [(i, i ^ bit) for i in range(size)])]
    ppermute x0 -> x11, starting transfers between devices: none -> 13.4 us  [swap(): return lax.ppermute(value, AXIS, [(i, i ^ bit) for i in range(size)])]
    dot_general x1 -> x0, matrix products: 10.3 us -> none  [conv_by_inputs(): lax.dot_general(flat, columns, (((0,), (0,)), ((), ())), preferred_elemen...]
    pallas_call x0 -> x4, Pallas kernels: none -> 9.66 us  [partials(): pl.pallas_call(functools.partial(partial_kernel, m, first), in_specs=[vme...]
    reshape x2 -> x0, local copies, waits for them, and re-layouts: 5.43 us -> none  [the longest x1 5.26 us: make_patches(): jnp.transpose(joined, (0, 2, 1, 3, 4)).reshape(9 * depth, count * 256)]
    transpose x1 -> x0, local copies, waits for them, and re-layouts: 4.06 us -> none  [make_patches(): jnp.transpose(joined, (0, 2, 1, 3, 4)).reshape(9 * depth, count * 256)]
    unnamed x15 -> x10, local copies, waits for them, and re-layouts: 9.3 us -> 5.59 us
  transfers between devices with their start and end apart: 1 -> 11, of which waited for: 1 -> 4; matrix products, arithmetic and copies ran while one was open for 0% -> 1% of each run, Pallas kernels for 0% -> 14%
where the time goes in v1:
time: 48.3 us; the launch traced here: 48.1 us
  waiting for transfers between devices  17.8 us (37%)
  starting transfers between devices  13.4 us (28%)
  Pallas kernels  9.66 us (20%)
  local copies, waits for them, and re-layouts  5.59 us (12%)
  other arithmetic  1.45 us (3%)
    ppermute x11, waiting for transfers between devices, swap(): return lax.ppermute(value, AXIS, [(i, i ^ bit) for i in range(size)])  17.8 us
    ppermute x11, starting transfers between devices, swap(): return lax.ppermute(value, AXIS, [(i, i ^ bit) for i in range(size)])  13.4 us
    pallas_call x4, Pallas kernels, partials(): pl.pallas_call(functools.partial(partial_kernel, m, first), in_specs=[vme...  9.66 us
    unnamed x10, local copies, waits for them, and re-layouts  5.59 us
  transfers between devices with their start and end apart: 11, of which 4 were waited for; matrix products, arithmetic and copies ran while one was open for 1% of the time, Pallas kernels for 14%

profile of v1, /device:TPU:0, one launch (start us, length us, event | category | flops | bytes accessed | tf_op | source)
XLA Modules:
  0.0 48.1 jit_solution(11583506502103128594)
XLA Ops:
  0.0 4.0 %copy-done = bf16[1,9,192,3072]{3,2,1,0:T(8,128)(2,1)S(1)} copy-done((bf16[1,9,192,3072]{3,2,1,0:T(8,128)(2,1)S(1)}, bf16[1,9,192,3072]{3,2,1,0:T(8,128)(2,1)}, u32[]{:S(2)}) %copy-start) | copy-done | bytes 10616856
  4.0 0.9 %copy-done.2 = bf16[2,192,256]{2,1,0:T(8,128)(2,1)S(1)} copy-done((bf16[2,192,256]{2,1,0:T(8,128)(2,1)S(1)}, bf16[2,192,256]{2,1,0:T(8,128)(2,1)}, u32[]{:S(2)}) %copy-start.2) | copy-done | bytes 196632
  4.9 2.8 %partials_3.1 = (bf16[1728,512]{1,0:T(8,128)(2,1)S(1)}, f32[2,192,512]{2,1,0:T(8,128)S(1)}, f32[2,192,512]{2,1,0:T(8,128)S(1)}) custom-call(bf16[2,192,256]{2,1,0:T(8,128)(2,1)S(1)} %copy-done.2, bf16[1728,3072]{1,0:T(8,128)(2,1)S(1)} %bitcast.55), custom_call_target="tpu_custom_call" | custom-call | flops 1358954496 | bytes 2654208 | tf_op jit(solution)/shard_map/partials_3/pallas_call | solution.py:106
  7.8 0.6 %collective-permute-start.7 = (f32[2,192,512]{2,1,0:T(8,128)S(1)}, f32[2,192,512]{2,1,0:T(8,128)S(1)}, u32[]{:S(2)}, u32[]{:S(2)}) collective-permute-start(f32[2,192,512]{2,1,0:T(8,128)S(1)} %get-tuple-element.22), channel_id=1, source_target_pairs={{0,1},{1,0},{2,3},{3,2},{4,5},{5,4},{6,7},{7,6},{8,9},{9,8},{10,11... | collective-permute-start | bytes 2359304 | tf_op jit(solution)/shard_map/ppermute | solution.py:127
  8.3 0.6 %copy-done.1 = bf16[1,9,192,3072]{3,2,1,0:T(8,128)(2,1)S(1)} copy-done((bf16[1,9,192,3072]{3,2,1,0:T(8,128)(2,1)S(1)}, bf16[1,9,192,3072]{3,2,1,0:T(8,128)(2,1)}, u32[]{:S(2)}) %copy-start.1) | copy-done | bytes 10616856
  9.0 2.3 %partials_2.1 = (f32[2,192,512]{2,1,0:T(8,128)S(1)}, f32[2,192,512]{2,1,0:T(8,128)S(1)}) custom-call(bf16[1728,512]{1,0:T(8,128)(2,1)S(1)} %get-tuple-element.14.source, bf16[1728,3072]{1,0:T(8,128)(2,1)S(1)} %bitcast.56), custom_call_target="tpu_custom_call" | custom-call | flops 1358954496 | bytes 2654208 | tf_op jit(solution)/shard_map/partials_2/pallas_call | solution.py:106
  11.3 0.5 %collective-permute-start.5 = (f32[2,192,512]{2,1,0:T(8,128)S(1)}, f32[2,192,512]{2,1,0:T(8,128)S(1)}, u32[]{:S(2)}, u32[]{:S(2)}) collective-permute-start(f32[2,192,512]{2,1,0:T(8,128)S(1)} %get-tuple-element.20), channel_id=1, source_target_pairs={{0,1},{1,0},{2,3},{3,2},{4,5},{5,4},{6,7},{7,6},{8,9},{9,8},{10,11... | collective-permute-start | bytes 2359304 | tf_op jit(solution)/shard_map/ppermute | solution.py:127
  11.8 2.3 %partials_1.1 = (f32[2,192,512]{2,1,0:T(8,128)S(1)}, f32[2,192,512]{2,1,0:T(8,128)S(1)}) custom-call(bf16[1728,512]{1,0:T(8,128)(2,1)S(1)} %get-tuple-element.14.source, bf16[1728,3072]{1,0:T(8,128)(2,1)S(1)} %bitcast.57), custom_call_target="tpu_custom_call" | custom-call | flops 1358954496 | bytes 2654208 | tf_op jit(solution)/shard_map/partials_1/pallas_call | solution.py:106
  14.1 0.1 collective-permute-start.2
  14.3 2.3 %partials_0.1 = (f32[2,192,512]{2,1,0:T(8,128)S(1)}, f32[2,192,512]{2,1,0:T(8,128)S(1)}) custom-call(bf16[1728,512]{1,0:T(8,128)(2,1)S(1)} %get-tuple-element.14.source, bf16[1728,3072]{1,0:T(8,128)(2,1)S(1)} %bitcast.58), custom_call_target="tpu_custom_call" | custom-call | flops 1358954496 | bytes 2654208 | tf_op jit(solution)/shard_map/partials_0/pallas_call | solution.py:106
  16.5 0.5 %collective-permute-start = (f32[2,192,512]{2,1,0:T(8,128)S(1)}, f32[2,192,512]{2,1,0:T(8,128)S(1)}, u32[]{:S(2)}, u32[]{:S(2)}) collective-permute-start(f32[2,192,512]{2,1,0:T(8,128)S(1)} %get-tuple-element.16), channel_id=1, source_target_pairs={{0,1},{1,0},{2,3},{3,2},{4,5},{5,4},{6,7},{7,6},{8,9},{9,8},{10,11... | collective-permute-start | bytes 2359304 | tf_op jit(solution)/shard_map/ppermute | solution.py:127
  17.2 2.6 %collective-permute-start.8 = (f16[192,512]{1,0:T(8,128)(2,1)S(1)}, f16[192,512]{1,0:T(8,128)(2,1)S(1)}, u32[]{:S(2)}, u32[]{:S(2)}) collective-permute-start(f16[192,512]{1,0:T(8,128)(2,1)S(1)} %fusion.25), channel_id=1, source_target_pairs={{0,2},{1,3},{2,0},{3,1},{4,6},{5,7},{6,4},{7,5},{8,10},{9,11},{10,... | collective-permute-start | bytes 589832 | tf_op jit(solution)/shard_map/ppermute | solution.py:127
  20.0 2.1 %collective-permute-start.3 = (f16[192,512]{1,0:T(8,128)(2,1)S(1)}, f16[192,512]{1,0:T(8,128)(2,1)S(1)}, u32[]{:S(2)}, u32[]{:S(2)}) collective-permute-start(f16[192,512]{1,0:T(8,128)(2,1)S(1)} %fusion.23), channel_id=1, source_target_pairs={{0,2},{1,3},{2,0},{3,1},{4,6},{5,7},{6,4},{7,5},{8,10},{9,11},{10,... | collective-permute-start | bytes 589832 | tf_op jit(solution)/shard_map/ppermute | solution.py:127
  22.3 3.3 %collective-permute-done.8 = f16[192,512]{1,0:T(8,128)(2,1)S(1)} collective-permute-done((f16[192,512]{1,0:T(8,128)(2,1)S(1)}, f16[192,512]{1,0:T(8,128)(2,1)S(1)}, u32[]{:S(2)}, u32[]{:S(2)}) %collective-permute-start.8) | collective-permute-done | bytes 196640 | tf_op jit(solution)/shard_map/ppermute | solution.py:127
  25.5 0.1 fusion.5
  25.6 2.1 %collective-permute-start.9 = (f16[192,512]{1,0:T(8,128)(2,1)S(1)}, f16[192,512]{1,0:T(8,128)(2,1)S(1)}, u32[]{:S(2)}, u32[]{:S(2)}) collective-permute-start(f16[192,512]{1,0:T(8,128)(2,1)S(1)} %fusion.5), channel_id=1, source_target_pairs={{0,4},{1,5},{2,6},{3,7},{4,0},{5,1},{6,2},{7,3},{8,12},{9,13},{10,... | collective-permute-start | bytes 589832 | tf_op jit(solution)/shard_map/ppermute | solution.py:127
  27.7 6.3 %collective-permute-done.3 = f16[192,512]{1,0:T(8,128)(2,1)S(1)} collective-permute-done((f16[192,512]{1,0:T(8,128)(2,1)S(1)}, f16[192,512]{1,0:T(8,128)(2,1)S(1)}, u32[]{:S(2)}, u32[]{:S(2)}) %collective-permute-start.3) | collective-permute-done | bytes 196640 | tf_op jit(solution)/shard_map/ppermute | solution.py:127
  34.1 2.1 %collective-permute-start.4 = (f16[192,512]{1,0:T(8,128)(2,1)S(1)}, f16[192,512]{1,0:T(8,128)(2,1)S(1)}, u32[]{:S(2)}, u32[]{:S(2)}) collective-permute-start(f16[192,512]{1,0:T(8,128)(2,1)S(1)} %fusion.14), channel_id=1, source_target_pairs={{0,4},{1,5},{2,6},{3,7},{4,0},{5,1},{6,2},{7,3},{8,12},{9,13},{10,... | collective-permute-start | bytes 589832 | tf_op jit(solution)/shard_map/ppermute | solution.py:127
  36.1 0.1 fusion.10
  36.2 2.7 %collective-permute-start.10 = (f16[192,512]{1,0:T(8,128)(2,1)S(1)}, f16[192,512]{1,0:T(8,128)(2,1)S(1)}, u32[]{:S(2)}, u32[]{:S(2)}) collective-permute-start(f16[192,512]{1,0:T(8,128)(2,1)S(1)} %fusion.10), channel_id=1, source_target_pairs={{0,8},{1,9},{2,10},{3,11},{4,12},{5,13},{6,14},{7,15},{8,0},{9,1},... | collective-permute-start | bytes 589832 | tf_op jit(solution)/shard_map/ppermute | solution.py:127
  38.9 5.3 %collective-permute-done.4 = f16[192,512]{1,0:T(8,128)(2,1)S(1)} collective-permute-done((f16[192,512]{1,0:T(8,128)(2,1)S(1)}, f16[192,512]{1,0:T(8,128)(2,1)S(1)}, u32[]{:S(2)}, u32[]{:S(2)}) %collective-permute-start.4) | collective-permute-done | bytes 196640 | tf_op jit(solution)/shard_map/ppermute | solution.py:127
  44.3 3.0 %collective-permute-done.10 = f16[192,512]{1,0:T(8,128)(2,1)S(1)} collective-permute-done((f16[192,512]{1,0:T(8,128)(2,1)S(1)}, f16[192,512]{1,0:T(8,128)(2,1)S(1)}, u32[]{:S(2)}, u32[]{:S(2)}) %collective-permute-start.10) | collective-permute-done | bytes 196640 | tf_op jit(solution)/shard_map/ppermute | solution.py:127
  47.2 0.1 fusion.21
  47.3 0.7 %fusion.1 = bf16[2,192,256]{2,1,0:T(8,128)(2,1)} fusion(f32[24,2,8,256]{3,2,1,0:T(8,128)S(1)} %bitcast.59, bf16[2,192,256]{2,1,0:T(8,128)(2,1)S(1)} %copy-done.3), kind=kLoop, calls=%fused_computation.2 | loop fusion | flops 294912 | bytes 786432 | tf_op jit(solution)/shard_map/convert_element_type | solution.py:29
  (21 shorter events, 0.6 us)
Async XLA Ops:
  0.0 4.0 %copy-start = (bf16[1,9,192,3072]{3,2,1,0:T(8,128)(2,1)S(1)}, bf16[1,9,192,3072]{3,2,1,0:T(8,128)(2,1)}, u32[]{:S(2)}) copy-start(bf16[1,9,192,3072]{3,2,1,0:T(8,128)(2,1)} %param.4) | copy-start | bytes 31850500
  4.0 0.9 %copy-start.2 = (bf16[2,192,256]{2,1,0:T(8,128)(2,1)S(1)}, bf16[2,192,256]{2,1,0:T(8,128)(2,1)}, u32[]{:S(2)}) copy-start(bf16[2,192,256]{2,1,0:T(8,128)(2,1)} %source.1) | copy-start | bytes 589828
  4.9 4.0 %copy-start.1 = (bf16[1,9,192,3072]{3,2,1,0:T(8,128)(2,1)S(1)}, bf16[1,9,192,3072]{3,2,1,0:T(8,128)(2,1)}, u32[]{:S(2)}) copy-start(bf16[1,9,192,3072]{3,2,1,0:T(8,128)(2,1)} %param.4) | copy-start | bytes 31850500
  7.8 9.3 %collective-permute-start.7 = (f32[2,192,512]{2,1,0:T(8,128)S(1)}, f32[2,192,512]{2,1,0:T(8,128)S(1)}, u32[]{:S(2)}, u32[]{:S(2)}) collective-permute-start(f32[2,192,512]{2,1,0:T(8,128)S(1)} %get-tuple-element.22), channel_id=1, source_target_pairs={{0,1},{1,0},{2,3},{3,2},{4,5},{5,4},{6,7},{7,6},{8,9},{9,8},{10,11... | collective-permute-start | bytes 2359304 | tf_op jit(solution)/shard_map/ppermute | solution.py:127
  11.3 8.5 %collective-permute-start.5 = (f32[2,192,512]{2,1,0:T(8,128)S(1)}, f32[2,192,512]{2,1,0:T(8,128)S(1)}, u32[]{:S(2)}, u32[]{:S(2)}) collective-permute-start(f32[2,192,512]{2,1,0:T(8,128)S(1)} %get-tuple-element.20), channel_id=1, source_target_pairs={{0,1},{1,0},{2,3},{3,2},{4,5},{5,4},{6,7},{7,6},{8,9},{9,8},{10,11... | collective-permute-start | bytes 2359304 | tf_op jit(solution)/shard_map/ppermute | solution.py:127
  14.1 33.1 %copy-start.4 = (f32[1,192]{1,0:T(1,128)S(1)}, f32[1,192]{1,0:T(1,128)}, u32[]{:S(2)}) copy-start(f32[1,192]{1,0:T(1,128)} %param.5) | copy-start | bytes 2308
  14.1 33.2 %copy-start.3 = (bf16[2,192,256]{2,1,0:T(8,128)(2,1)S(1)}, bf16[2,192,256]{2,1,0:T(8,128)(2,1)}, u32[]{:S(2)}) copy-start(bf16[2,192,256]{2,1,0:T(8,128)(2,1)} %source.1) | copy-start | bytes 589828
  14.1 5.8 %collective-permute-start.2 = (f32[2,192,512]{2,1,0:T(8,128)S(1)}, f32[2,192,512]{2,1,0:T(8,128)S(1)}, u32[]{:S(2)}, u32[]{:S(2)}) collective-permute-start(f32[2,192,512]{2,1,0:T(8,128)S(1)} %get-tuple-element.18), channel_id=1, source_target_pairs={{0,1},{1,0},{2,3},{3,2},{4,5},{5,4},{6,7},{7,6},{8,9},{9,8},{10,11... | collective-permute-start | bytes 2359304 | tf_op jit(solution)/shard_map/ppermute | solution.py:127
  16.5 5.6 %collective-permute-start = (f32[2,192,512]{2,1,0:T(8,128)S(1)}, f32[2,192,512]{2,1,0:T(8,128)S(1)}, u32[]{:S(2)}, u32[]{:S(2)}) collective-permute-start(f32[2,192,512]{2,1,0:T(8,128)S(1)} %get-tuple-element.16), channel_id=1, source_target_pairs={{0,1},{1,0},{2,3},{3,2},{4,5},{5,4},{6,7},{7,6},{8,9},{9,8},{10,11... | collective-permute-start | bytes 2359304 | tf_op jit(solution)/shard_map/ppermute | solution.py:127
  17.2 8.4 %collective-permute-start.8 = (f16[192,512]{1,0:T(8,128)(2,1)S(1)}, f16[192,512]{1,0:T(8,128)(2,1)S(1)}, u32[]{:S(2)}, u32[]{:S(2)}) collective-permute-start(f16[192,512]{1,0:T(8,128)(2,1)S(1)} %fusion.25), channel_id=1, source_target_pairs={{0,2},{1,3},{2,0},{3,1},{4,6},{5,7},{6,4},{7,5},{8,10},{9,11},{10,... | collective-permute-start | bytes 589832 | tf_op jit(solution)/shard_map/ppermute | solution.py:127
  19.9 16.3 %collective-permute-start.6 = (f16[192,512]{1,0:T(8,128)(2,1)S(1)}, f16[192,512]{1,0:T(8,128)(2,1)S(1)}, u32[]{:S(2)}, u32[]{:S(2)}) collective-permute-start(f16[192,512]{1,0:T(8,128)(2,1)S(1)} %fusion.24), channel_id=1, source_target_pairs={{0,2},{1,3},{2,0},{3,1},{4,6},{5,7},{6,4},{7,5},{8,10},{9,11},{10,... | collective-permute-start | bytes 589832 | tf_op jit(solution)/shard_map/ppermute | solution.py:127
  20.0 13.9 %collective-permute-start.3 = (f16[192,512]{1,0:T(8,128)(2,1)S(1)}, f16[192,512]{1,0:T(8,128)(2,1)S(1)}, u32[]{:S(2)}, u32[]{:S(2)}) collective-permute-start(f16[192,512]{1,0:T(8,128)(2,1)S(1)} %fusion.23), channel_id=1, source_target_pairs={{0,2},{1,3},{2,0},{3,1},{4,6},{5,7},{6,4},{7,5},{8,10},{9,11},{10,... | collective-permute-start | bytes 589832 | tf_op jit(solution)/shard_map/ppermute | solution.py:127
  22.2 16.8 %collective-permute-start.1 = (f16[192,512]{1,0:T(8,128)(2,1)S(1)}, f16[192,512]{1,0:T(8,128)(2,1)S(1)}, u32[]{:S(2)}, u32[]{:S(2)}) collective-permute-start(f16[192,512]{1,0:T(8,128)(2,1)S(1)} %fusion.22), channel_id=1, source_target_pairs={{0,2},{1,3},{2,0},{3,1},{4,6},{5,7},{6,4},{7,5},{8,10},{9,11},{10,... | collective-permute-start | bytes 589832 | tf_op jit(solution)/shard_map/ppermute | solution.py:127
  25.6 10.5 %collective-permute-start.9 = (f16[192,512]{1,0:T(8,128)(2,1)S(1)}, f16[192,512]{1,0:T(8,128)(2,1)S(1)}, u32[]{:S(2)}, u32[]{:S(2)}) collective-permute-start(f16[192,512]{1,0:T(8,128)(2,1)S(1)} %fusion.5), channel_id=1, source_target_pairs={{0,4},{1,5},{2,6},{3,7},{4,0},{5,1},{6,2},{7,3},{8,12},{9,13},{10,... | collective-permute-start | bytes 589832 | tf_op jit(solution)/shard_map/ppermute | solution.py:127
  34.1 10.2 %collective-permute-start.4 = (f16[192,512]{1,0:T(8,128)(2,1)S(1)}, f16[192,512]{1,0:T(8,128)(2,1)S(1)}, u32[]{:S(2)}, u32[]{:S(2)}) collective-permute-start(f16[192,512]{1,0:T(8,128)(2,1)S(1)} %fusion.14), channel_id=1, source_target_pairs={{0,4},{1,5},{2,6},{3,7},{4,0},{5,1},{6,2},{7,3},{8,12},{9,13},{10,... | collective-permute-start | bytes 589832 | tf_op jit(solution)/shard_map/ppermute | solution.py:127
  36.2 11.0 %collective-permute-start.10 = (f16[192,512]{1,0:T(8,128)(2,1)S(1)}, f16[192,512]{1,0:T(8,128)(2,1)S(1)}, u32[]{:S(2)}, u32[]{:S(2)}) collective-permute-start(f16[192,512]{1,0:T(8,128)(2,1)S(1)} %fusion.10), channel_id=1, source_target_pairs={{0,8},{1,9},{2,10},{3,11},{4,12},{5,13},{6,14},{7,15},{8,0},{9,1},... | collective-permute-start | bytes 589832 | tf_op jit(solution)/shard_map/ppermute | solution.py:127

commit v2 on v0

v2 whole, which is shorter than its diff:
```python
import functools
import math

import jax
import jax.numpy as jnp
from jax import lax
from jax.experimental import pallas as pl
from jax.experimental.pallas import tpu as pltpu
from jax.sharding import PartitionSpec as P

AXIS = "chan"
SENT = jnp.float16


def make_patches(stack):
    count, depth, pixels = stack.shape
    side = math.isqrt(pixels)
    images = stack.reshape(count, depth, side, side)
    padded = jnp.pad(images, ((0, 0), (0, 0), (1, 1), (1, 1)))
    shifted = [padded[:, :, row : row + side, col : col + side] for row in range(3) for col in range(3)]
    joined = jnp.stack(shifted, 0)
    return jnp.transpose(joined, (0, 2, 1, 3, 4)).reshape(9 * depth, count * pixels)


def conv_plain(stack, flat, layer_bias):
    count, owned, pixels = stack.shape
    total = lax.psum_scatter(
        lax.dot_general(flat, make_patches(stack), (((0,), (0,)), ((), ())), preferred_element_type=jnp.float32),
        AXIS,
        scatter_dimension=0,
        tiled=True,
    )
    activated = jnp.maximum(total + layer_bias[:, None], 0.0)
    activated = jnp.transpose(activated.reshape(owned, count, pixels), (1, 0, 2))
    return (stack.astype(jnp.float32) + activated).astype(jnp.bfloat16)


def write_patches(maps_ref, x_ref):
    count, depth, pixels = maps_ref.shape
    side = math.isqrt(pixels)
    lane = lax.broadcasted_iota(jnp.int32, (depth, pixels), 1)
    row, col = lane // side, lane % side
    for image in range(count):
        plain = maps_ref[image]
        wide = plain.astype(jnp.float32)
        for tap in range(9):
            dy, dx = tap // 3 - 1, tap % 3 - 1
            shift = dy * side + dx
            value = plain
            if shift:
                value = pltpu.roll(wide, (-shift) % pixels, 1)
                for step, place in ((dy, row), (dx, col)):
                    if step > 0:
                        value = jnp.where(place < side - 1, value, 0.0)
                    elif step < 0:
                        value = jnp.where(place > 0, value, 0.0)
                value = value.astype(jnp.bfloat16)
            x_ref[tap * depth : (tap + 1) * depth, image * pixels : (image + 1) * pixels] = value


def contribution(x_ref, weights, low, out_ref):
    _, count, owned, pixels = out_ref.shape
    part = lax.dot_general(weights, x_ref[...], (((0,), (0,)), ((), ())), preferred_element_type=jnp.float32)
    for core in range(2):
        for image in range(count):
            rows, at = slice(core * owned, (core + 1) * owned), slice(image * pixels, (image + 1) * pixels)
            out_ref[low ^ core, image] = part[rows, at]


def columns_of(distance, width):
    pair = lax.div(lax.axis_index(AXIS), 2)
    return pl.ds(pl.multiple_of((pair ^ distance) * width, 128), width)


def first_kernel(distances, maps_ref, w_ref, x_ref, out_ref, maps_buf, w_buf, sems):
    low = lax.rem(lax.axis_index(AXIS), 2)
    maps_copy = pltpu.make_async_copy(maps_ref, maps_buf, sems.at[0])
    maps_copy.start()
    copies = []
    for at, distance in enumerate(distances):
        columns = columns_of(distance, w_buf.shape[2])
        copies.append(pltpu.make_async_copy(w_ref.at[:, columns], w_buf.at[at], sems.at[1 + at]))
        copies[-1].start()
    maps_copy.wait()
    write_patches(maps_buf, x_ref)
    for at, copy in enumerate(copies):
        copy.wait()
        contribution(x_ref, w_buf[at], low, out_ref.at[:, at])


def next_kernel(distances, x_ref, w_ref, out_ref):
    low = lax.rem(lax.axis_index(AXIS), 2)
    width = 2 * out_ref.shape[3]
    for at, distance in enumerate(distances):
        contribution(x_ref, w_ref[:, columns_of(distance, width)], low, out_ref.at[:, at])


def partials(distances, source, flat, shape, first=False):
    count, owned, pixels = shape
    depth = flat.shape[0]
    sums = jax.ShapeDtypeStruct((2, len(distances), count, owned, pixels), jnp.float32)
    patches = jax.ShapeDtypeStruct((depth, count * pixels), jnp.bfloat16)
    vmem, hbm = pl.BlockSpec(memory_space=pltpu.VMEM), pl.BlockSpec(memory_space=pltpu.HBM)
    scratch = []
    if first:
        source = pltpu.with_memory_space_constraint(source, pltpu.HBM)
        flat = pltpu.with_memory_space_constraint(flat, pltpu.HBM)
        scratch = [
            pltpu.VMEM(shape, jnp.bfloat16),
            pltpu.VMEM((len(distances), depth, 2 * owned), jnp.bfloat16),
            pltpu.SemaphoreType.DMA((1 + len(distances),)),
        ]
    return pl.pallas_call(
        functools.partial(first_kernel if first else next_kernel, distances),
        in_specs=[hbm, hbm] if first else [vmem, vmem],
        out_specs=[vmem] * 2 if first else vmem,
        out_shape=[patches, sums] if first else sums,
        scratch_shapes=scratch,
        compiler_params=pltpu.CompilerParams(vmem_limit_bytes=24 * 2**20),
        cost_estimate=pl.CostEstimate(
            flops=4 * depth * len(distances) * owned * count * pixels,
            bytes_accessed=4 * depth * len(distances) * owned,
            transcendentals=0,
        ),
        name="partials_" + "_".join(map(str, distances)),
    )(source, flat)


def conv_halving(stack, flat, layer_bias):
    shape = stack.shape
    images = range(shape[0])
    size = lax.axis_size(AXIS)

    def swap(value, bits):
        return lax.ppermute(value, AXIS, [(i, i ^ bits) for i in range(size)])

    def wide(value):
        return value.astype(jnp.float32)

    def core_sums(distances, out):
        came = swap(out[1].astype(SENT), 1)
        return {d: [out[0, at, i] + wide(came[at, i]) for i in images] for at, d in enumerate(distances)}

    def across(sums, distance):
        return swap(jnp.stack([value.astype(SENT) for value in sums]), 2 * distance)

    far, near = (7, 6, 5, 4), (3, 2, 1, 0)
    patches, out = partials(far, stack, flat, shape, first=True)
    later = partials(near, patches, flat, shape)
    sums = core_sums(far, out)
    came = [across(sums[d], d - 4) for d in (5, 6, 7)]
    kept = [sums[4][i] + sum(wide(c[i]) for c in came) for i in images]
    sums = core_sums(near, later)
    came = [across(sums[d], d) for d in (1, 2, 3)]
    came.append(across(kept, 4))
    bias = layer_bias[:, None]
    total = [sums[0][i] + sum(wide(c[i]) for c in came) for i in images]
    return jnp.stack([(wide(stack[i]) + jnp.maximum(total[i] + bias, 0.0)).astype(jnp.bfloat16) for i in images])


def local(size, maps, kernels, bias):
    for layer in range(kernels.shape[0]):
        owned = maps.shape[1]
        flat = kernels[layer].reshape(9 * owned, kernels.shape[3])
        if size == 16 and owned % 64 == 0 and maps.shape[2] % 128 == 0:
            maps = conv_halving(maps, flat, bias[layer])
        else:
            maps = conv_plain(maps, flat, bias[layer])
    return maps


def solution(mesh):
    in_specs = (P("groups", AXIS, None), P(None, None, AXIS, None), P(None, AXIS))
    out_specs = P("groups", AXIS, None)
    return jax.shard_map(
        functools.partial(local, mesh.shape[AXIS]), mesh=mesh, in_specs=in_specs, out_specs=out_specs, check_vma=False
    )
```

time: 132 us -> 38.4 us (0.29)
  waiting for transfers between devices: 88.1 us -> 14.3 us
  local copies, waits for them, and re-layouts: 18.9 us -> 0.02 us
  starting transfers between devices: 0.01 us -> 13.5 us
  between operations: 13.5 us -> 0.11 us
  matrix products: 10.3 us -> 0 us
  Pallas kernels: 0 us -> 8.32 us
    unnamed x2 -> x0, waiting for transfers between devices: 88.1 us -> none
    ppermute x0 -> x9, waiting for transfers between devices: none -> 14.3 us  [swap(): return lax.ppermute(value, AXIS, [(i, i ^ bits) for i in range(size)])]
    ppermute x0 -> x9, starting transfers between devices: none -> 13.5 us  [swap(): return lax.ppermute(value, AXIS, [(i, i ^ bits) for i in range(size)])]
    dot_general x1 -> x0, matrix products: 10.3 us -> none  [conv_by_inputs(): lax.dot_general(flat, columns, (((0,), (0,)), ((), ())), preferred_elemen...]
    unnamed x15 -> x6, local copies, waits for them, and re-layouts: 9.3 us -> 0.02 us
    pallas_call x0 -> x2, Pallas kernels: none -> 8.32 us  [partials(): pl.pallas_call(functools.partial(first_kernel if first else next_kernel,...]
    reshape x2 -> x0, local copies, waits for them, and re-layouts: 5.43 us -> none  [the longest x1 5.26 us: make_patches(): jnp.transpose(joined, (0, 2, 1, 3, 4)).reshape(9 * depth, count * 256)]
    transpose x1 -> x0, local copies, waits for them, and re-layouts: 4.06 us -> none  [make_patches(): jnp.transpose(joined, (0, 2, 1, 3, 4)).reshape(9 * depth, count * 256)]
  transfers between devices with their start and end apart: 1 -> 9, of which waited for: 1 -> 5; matrix products, arithmetic and copies ran while one was open for 0% -> 2% of each run, Pallas kernels for 0% -> 8%
where the time goes in v2:
time: 38.4 us; the launch traced here: 38.3 us
  waiting for transfers between devices  14.3 us (37%)
  starting transfers between devices  13.5 us (35%)
  Pallas kernels  8.32 us (22%)
  other arithmetic  1.95 us (5%)
    ppermute x9, waiting for transfers between devices, swap(): return lax.ppermute(value, AXIS, [(i, i ^ bits) for i in range(size)])  14.3 us
    ppermute x9, starting transfers between devices, swap(): return lax.ppermute(value, AXIS, [(i, i ^ bits) for i in range(size)])  13.5 us
    pallas_call x2, Pallas kernels, partials(): pl.pallas_call(functools.partial(first_kernel if first else next_kernel,...  8.32 us
  transfers between devices with their start and end apart: 9, of which 5 were waited for; matrix products, arithmetic and copies ran while one was open for 2% of the time, Pallas kernels for 8%

profile of v2, /device:TPU:0, one launch (start us, length us, event | category | flops | bytes accessed | tf_op | source)
XLA Modules:
  0.0 38.3 jit_solution(16931593753413776347)
XLA Ops:
  0.0 5.3 %partials_7_6_5_4.1 = (bf16[1728,512]{1,0:T(8,128)(2,1)S(1)}, f32[2,4,2,192,256]{4,3,2,1,0:T(8,128)S(1)}) custom-call(bf16[2,192,256]{2,1,0:T(8,128)(2,1)} %maps_ref.1, bf16[1728,3072]{1,0:T(8,128)(2,1)} %bitcast.166), custom_call_target="tpu_custom_call" | custom-call | flops 2717908992 | bytes 5308416 | tf_op jit(solution)/shard_map/partials_7_6_5_4/pallas_call | solution.py:113
  5.3 0.1 fusion.1
  5.4 0.5 %collective-permute-start.4 = (f16[4,2,192,256]{3,2,1,0:T(8,128)(2,1)S(1)}, f16[4,2,192,256]{3,2,1,0:T(8,128)(2,1)S(1)}, u32[]{:S(2)}, u32[]{:S(2)}) collective-permute-start(f16[4,2,192,256]{3,2,1,0:T(8,128)(2,1)S(1)} %fusion.1), channel_id=1, source_target_pairs={{0,1},{1,0},{2,3},{3,2},{4,5},{5,4},{6,7},{7,6},{8,9},{9,8},{10,11... | collective-permute-start | bytes 2359304 | tf_op jit(solution)/shard_map/ppermute | solution.py:135
  5.9 3.1 %partials_3_2_1_0.1 = f32[2,4,2,192,256]{4,3,2,1,0:T(8,128)S(1)} custom-call(bf16[1728,512]{1,0:T(8,128)(2,1)S(1)} %get-tuple-element.7.x_ref, bf16[1728,3072]{1,0:T(8,128)(2,1)S(1)} %bitcast.167), custom_call_target="tpu_custom_call" | custom-call | flops 2717908992 | bytes 5308416 | tf_op jit(solution)/shard_map/partials_3_2_1_0/pallas_call | solution.py:113
  9.0 0.1 fusion
  9.1 0.3 collective-permute-start
  9.5 0.2 fusion.33
  9.6 0.1 pad_maximum_fusion.4
  9.7 2.9 %collective-permute-start.6 = (f16[2,192,256]{2,1,0:T(8,128)(2,1)S(1)}, f16[2,192,256]{2,1,0:T(8,128)(2,1)S(1)}, u32[]{:S(2)}, u32[]{:S(2)}) collective-permute-start(f16[2,192,256]{2,1,0:T(8,128)(2,1)S(1)} %pad_maximum_fusion.4), channel_id=1, source_target_pairs={{0,4},{1,5},{2,6},{3,7},{4,0},{5,1},{6,2},{7,3},{8,12},{9,13},{10,... | collective-permute-start | bytes 589832 | tf_op jit(solution)/shard_map/ppermute | solution.py:135
  12.7 1.5 %collective-permute-start.7 = (f16[2,192,256]{2,1,0:T(8,128)(2,1)S(1)}, f16[2,192,256]{2,1,0:T(8,128)(2,1)S(1)}, u32[]{:S(2)}, u32[]{:S(2)}) collective-permute-start(f16[2,192,256]{2,1,0:T(8,128)(2,1)S(1)} %pad_maximum_fusion.5), channel_id=1, source_target_pairs={{0,6},{1,7},{2,4},{3,5},{4,2},{5,3},{6,0},{7,1},{8,14},{9,15},{10,... | collective-permute-start | bytes 589832 | tf_op jit(solution)/shard_map/ppermute | solution.py:135
  14.2 0.2 collective-permute-start.5
  14.4 0.2 fusion.19
  14.6 2.0 %collective-permute-start.2 = (f16[2,192,256]{2,1,0:T(8,128)(2,1)S(1)}, f16[2,192,256]{2,1,0:T(8,128)(2,1)S(1)}, u32[]{:S(2)}, u32[]{:S(2)}) collective-permute-start(f16[2,192,256]{2,1,0:T(8,128)(2,1)S(1)} %pad_maximum_fusion.1), channel_id=1, source_target_pairs={{0,4},{1,5},{2,6},{3,7},{4,0},{5,1},{6,2},{7,3},{8,12},{9,13},{10,... | collective-permute-start | bytes 589832 | tf_op jit(solution)/shard_map/ppermute | solution.py:135
  16.7 1.5 %collective-permute-start.3 = (f16[2,192,256]{2,1,0:T(8,128)(2,1)S(1)}, f16[2,192,256]{2,1,0:T(8,128)(2,1)S(1)}, u32[]{:S(2)}, u32[]{:S(2)}) collective-permute-start(f16[2,192,256]{2,1,0:T(8,128)(2,1)S(1)} %pad_maximum_fusion.2), channel_id=1, source_target_pairs={{0,6},{1,7},{2,4},{3,5},{4,2},{5,3},{6,0},{7,1},{8,14},{9,15},{10,... | collective-permute-start | bytes 589832 | tf_op jit(solution)/shard_map/ppermute | solution.py:135
  18.2 0.1 collective-permute-done.6
  18.3 2.0 %collective-permute-start.1 = (f16[2,192,256]{2,1,0:T(8,128)(2,1)S(1)}, f16[2,192,256]{2,1,0:T(8,128)(2,1)S(1)}, u32[]{:S(2)}, u32[]{:S(2)}) collective-permute-start(f16[2,192,256]{2,1,0:T(8,128)(2,1)S(1)} %pad_maximum_fusion), channel_id=1, source_target_pairs={{0,2},{1,3},{2,0},{3,1},{4,6},{5,7},{6,4},{7,5},{8,10},{9,11},{10,... | collective-permute-start | bytes 589832 | tf_op jit(solution)/shard_map/ppermute | solution.py:135
  20.3 3.7 %collective-permute-done.7 = f16[2,192,256]{2,1,0:T(8,128)(2,1)S(1)} collective-permute-done((f16[2,192,256]{2,1,0:T(8,128)(2,1)S(1)}, f16[2,192,256]{2,1,0:T(8,128)(2,1)S(1)}, u32[]{:S(2)}, u32[]{:S(2)}) %collective-permute-start.7) | collective-permute-done | bytes 196640 | tf_op jit(solution)/shard_map/ppermute | solution.py:135
  24.0 2.3 %collective-permute-done.5 = f16[2,192,256]{2,1,0:T(8,128)(2,1)S(1)} collective-permute-done((f16[2,192,256]{2,1,0:T(8,128)(2,1)S(1)}, f16[2,192,256]{2,1,0:T(8,128)(2,1)S(1)}, u32[]{:S(2)}, u32[]{:S(2)}) %collective-permute-start.5) | collective-permute-done | bytes 196640 | tf_op jit(solution)/shard_map/ppermute | solution.py:135
  26.3 0.1 fusion.35
  26.5 2.7 %collective-permute-start.8 = (f16[2,192,256]{2,1,0:T(8,128)(2,1)S(1)}, f16[2,192,256]{2,1,0:T(8,128)(2,1)S(1)}, u32[]{:S(2)}, u32[]{:S(2)}) collective-permute-start(f16[2,192,256]{2,1,0:T(8,128)(2,1)S(1)} %pad_maximum_fusion.6), channel_id=1, source_target_pairs={{0,8},{1,9},{2,10},{3,11},{4,12},{5,13},{6,14},{7,15},{8,0},{9,1},... | collective-permute-start | bytes 589832 | tf_op jit(solution)/shard_map/ppermute | solution.py:135
  29.1 6.8 %collective-permute-done.3 = f16[2,192,256]{2,1,0:T(8,128)(2,1)S(1)} collective-permute-done((f16[2,192,256]{2,1,0:T(8,128)(2,1)S(1)}, f16[2,192,256]{2,1,0:T(8,128)(2,1)S(1)}, u32[]{:S(2)}, u32[]{:S(2)}) %collective-permute-start.3) | collective-permute-done | bytes 196640 | tf_op jit(solution)/shard_map/ppermute | solution.py:135
  36.0 1.4 %collective-permute-done.8 = f16[2,192,256]{2,1,0:T(8,128)(2,1)S(1)} collective-permute-done((f16[2,192,256]{2,1,0:T(8,128)(2,1)S(1)}, f16[2,192,256]{2,1,0:T(8,128)(2,1)S(1)}, u32[]{:S(2)}, u32[]{:S(2)}) %collective-permute-start.8) | collective-permute-done | bytes 196640 | tf_op jit(solution)/shard_map/ppermute | solution.py:135
  37.4 0.2 fusion.25
  37.6 0.7 %pad_maximum_fusion.7 = bf16[2,192,256]{2,1,0:T(8,128)(2,1)} fusion(bf16[1,192,256]{2,1,0:T(8,128)(2,1)S(1)} %get-tuple-element.10, bf16[1,192,256]{2,1,0:T(8,128)(2,1)S(1)} %get-tuple-element.9), kind=kLoop, calls=%fused_computation.43 | loop fusion | flops 98304 | bytes 393216 | tf_op jit(solution)/shard_map/stack | solution.py:158
  (16 shorter events, 0.3 us)
Async XLA Ops:
  0.0 5.9 %copy-start = (bf16[1,9,192,3072]{3,2,1,0:T(8,128)(2,1)S(1)}, bf16[1,9,192,3072]{3,2,1,0:T(8,128)(2,1)}, u32[]{:S(2)}) copy-start(bf16[1,9,192,3072]{3,2,1,0:T(8,128)(2,1)} %param.4) | copy-start | bytes 31850500
  5.4 4.1 %collective-permute-start.4 = (f16[4,2,192,256]{3,2,1,0:T(8,128)(2,1)S(1)}, f16[4,2,192,256]{3,2,1,0:T(8,128)(2,1)S(1)}, u32[]{:S(2)}, u32[]{:S(2)}) collective-permute-start(f16[4,2,192,256]{3,2,1,0:T(8,128)(2,1)S(1)} %fusion.1), channel_id=1, source_target_pairs={{0,1},{1,0},{2,3},{3,2},{4,5},{5,4},{6,7},{7,6},{8,9},{9,8},{10,11... | collective-permute-start | bytes 2359304 | tf_op jit(solution)/shard_map/ppermute | solution.py:135
  9.1 5.2 %collective-permute-start = (f16[4,2,192,256]{3,2,1,0:T(8,128)(2,1)S(1)}, f16[4,2,192,256]{3,2,1,0:T(8,128)(2,1)S(1)}, u32[]{:S(2)}, u32[]{:S(2)}) collective-permute-start(f16[4,2,192,256]{3,2,1,0:T(8,128)(2,1)S(1)} %fusion), channel_id=1, source_target_pairs={{0,1},{1,0},{2,3},{3,2},{4,5},{5,4},{6,7},{7,6},{8,9},{9,8},{10,11... | collective-permute-start | bytes 2359304 | tf_op jit(solution)/shard_map/ppermute | solution.py:135
  9.7 27.7 %copy-start.1 = (bf16[2,192,256]{2,1,0:T(8,128)(2,1)S(1)}, bf16[2,192,256]{2,1,0:T(8,128)(2,1)}, u32[]{:S(2)}) copy-start(bf16[2,192,256]{2,1,0:T(8,128)(2,1)} %maps_ref.1) | copy-start | bytes 589828
  9.7 27.6 %copy-start.2 = (f32[1,192]{1,0:T(1,128)S(1)}, f32[1,192]{1,0:T(1,128)}, u32[]{:S(2)}) copy-start(f32[1,192]{1,0:T(1,128)} %param.5) | copy-start | bytes 2308
  9.7 8.6 %collective-permute-start.6 = (f16[2,192,256]{2,1,0:T(8,128)(2,1)S(1)}, f16[2,192,256]{2,1,0:T(8,128)(2,1)S(1)}, u32[]{:S(2)}, u32[]{:S(2)}) collective-permute-start(f16[2,192,256]{2,1,0:T(8,128)(2,1)S(1)} %pad_maximum_fusion.4), channel_id=1, source_target_pairs={{0,4},{1,5},{2,6},{3,7},{4,0},{5,1},{6,2},{7,3},{8,12},{9,13},{10,... | collective-permute-start | bytes 589832 | tf_op jit(solution)/shard_map/ppermute | solution.py:135
  12.7 11.3 %collective-permute-start.7 = (f16[2,192,256]{2,1,0:T(8,128)(2,1)S(1)}, f16[2,192,256]{2,1,0:T(8,128)(2,1)S(1)}, u32[]{:S(2)}, u32[]{:S(2)}) collective-permute-start(f16[2,192,256]{2,1,0:T(8,128)(2,1)S(1)} %pad_maximum_fusion.5), channel_id=1, source_target_pairs={{0,6},{1,7},{2,4},{3,5},{4,2},{5,3},{6,0},{7,1},{8,14},{9,15},{10,... | collective-permute-start | bytes 589832 | tf_op jit(solution)/shard_map/ppermute | solution.py:135
  14.2 12.1 %collective-permute-start.5 = (f16[2,192,256]{2,1,0:T(8,128)(2,1)S(1)}, f16[2,192,256]{2,1,0:T(8,128)(2,1)S(1)}, u32[]{:S(2)}, u32[]{:S(2)}) collective-permute-start(f16[2,192,256]{2,1,0:T(8,128)(2,1)S(1)} %pad_maximum_fusion.3), channel_id=1, source_target_pairs={{0,2},{1,3},{2,0},{3,1},{4,6},{5,7},{6,4},{7,5},{8,10},{9,11},{10,... | collective-permute-start | bytes 589832 | tf_op jit(solution)/shard_map/ppermute | solution.py:135
  14.6 14.5 %collective-permute-start.2 = (f16[2,192,256]{2,1,0:T(8,128)(2,1)S(1)}, f16[2,192,256]{2,1,0:T(8,128)(2,1)S(1)}, u32[]{:S(2)}, u32[]{:S(2)}) collective-permute-start(f16[2,192,256]{2,1,0:T(8,128)(2,1)S(1)} %pad_maximum_fusion.1), channel_id=1, source_target_pairs={{0,4},{1,5},{2,6},{3,7},{4,0},{5,1},{6,2},{7,3},{8,12},{9,13},{10,... | collective-permute-start | bytes 589832 | tf_op jit(solution)/shard_map/ppermute | solution.py:135
  16.7 19.3 %collective-permute-start.3 = (f16[2,192,256]{2,1,0:T(8,128)(2,1)S(1)}, f16[2,192,256]{2,1,0:T(8,128)(2,1)S(1)}, u32[]{:S(2)}, u32[]{:S(2)}) collective-permute-start(f16[2,192,256]{2,1,0:T(8,128)(2,1)S(1)} %pad_maximum_fusion.2), channel_id=1, source_target_pairs={{0,6},{1,7},{2,4},{3,5},{4,2},{5,3},{6,0},{7,1},{8,14},{9,15},{10,... | collective-permute-start | bytes 589832 | tf_op jit(solution)/shard_map/ppermute | solution.py:135
  18.3 17.7 %collective-permute-start.1 = (f16[2,192,256]{2,1,0:T(8,128)(2,1)S(1)}, f16[2,192,256]{2,1,0:T(8,128)(2,1)S(1)}, u32[]{:S(2)}, u32[]{:S(2)}) collective-permute-start(f16[2,192,256]{2,1,0:T(8,128)(2,1)S(1)} %pad_maximum_fusion), channel_id=1, source_target_pairs={{0,2},{1,3},{2,0},{3,1},{4,6},{5,7},{6,4},{7,5},{8,10},{9,11},{10,... | collective-permute-start | bytes 589832 | tf_op jit(solution)/shard_map/ppermute | solution.py:135
  26.5 10.9 %collective-permute-start.8 = (f16[2,192,256]{2,1,0:T(8,128)(2,1)S(1)}, f16[2,192,256]{2,1,0:T(8,128)(2,1)S(1)}, u32[]{:S(2)}, u32[]{:S(2)}) collective-permute-start(f16[2,192,256]{2,1,0:T(8,128)(2,1)S(1)} %pad_maximum_fusion.6), channel_id=1, source_target_pairs={{0,8},{1,9},{2,10},{3,11},{4,12},{5,13},{6,14},{7,15},{8,0},{9,1},... | collective-permute-start | bytes 589832 | tf_op jit(solution)/shard_map/ppermute | solution.py:135

commit v3 on v2

--- a/solution.py
+++ b/solution.py
@@ -72,58 +72,73 @@
     return pl.ds(pl.multiple_of((pair ^ distance) * width, 128), width)
 
 
-def first_kernel(distances, maps_ref, w_ref, x_ref, out_ref, maps_buf, w_buf, sems):
+def first_kernel(distances, rest, maps_ref, w_ref, x_ref, out_ref, rest_ref, maps_buf, w_buf, sems):
     low = lax.rem(lax.axis_index(AXIS), 2)
     maps_copy = pltpu.make_async_copy(maps_ref, maps_buf, sems.at[0])
     maps_copy.start()
     copies = []
-    for at, distance in enumerate(distances):
+    for at, distance in enumerate(distances + rest):
         columns = columns_of(distance, w_buf.shape[2])
-        copies.append(pltpu.make_async_copy(w_ref.at[:, columns], w_buf.at[at], sems.at[1 + at]))
+        target = w_buf.at[at] if at < len(distances) else rest_ref.at[at - len(distances)]
+        copies.append(pltpu.make_async_copy(w_ref.at[:, columns], target, sems.at[1 + at]))
         copies[-1].start()
     maps_copy.wait()
     write_patches(maps_buf, x_ref)
-    for at, copy in enumerate(copies):
+    for at, copy in enumerate(copies[: len(distances)]):
         copy.wait()
         contribution(x_ref, w_buf[at], low, out_ref.at[:, at])
-
-
-def next_kernel(distances, x_ref, w_ref, out_ref):
+    for copy in copies[len(distances) :]:
+        copy.wait()
+
+
+def next_kernel(x_ref, w_ref, before_ref, after_ref, out_ref):
     low = lax.rem(lax.axis_index(AXIS), 2)
-    width = 2 * out_ref.shape[3]
-    for at, distance in enumerate(distances):
-        contribution(x_ref, w_ref[:, columns_of(distance, width)], low, out_ref.at[:, at])
-
-
-def partials(distances, source, flat, shape, first=False):
+    for at in range(w_ref.shape[0]):
+        contribution(x_ref, w_ref[at], low, out_ref.at[:, at])
+
+
+def kernel_cost(depth, shape, chunks):
     count, owned, pixels = shape
+    return pl.CostEstimate(
+        flops=4 * depth * chunks * owned * count * pixels, bytes_accessed=4 * depth * chunks * owned, transcendentals=0
+    )
+
+
+def first_partials(distances, rest, stack, flat):
+    count, owned, pixels = stack.shape
     depth = flat.shape[0]
-    sums = jax.ShapeDtypeStruct((2, len(distances), count, owned, pixels), jnp.float32)
-    patches = jax.ShapeDtypeStruct((depth, count * pixels), jnp.bfloat16)
     vmem, hbm = pl.BlockSpec(memory_space=pltpu.VMEM), pl.BlockSpec(memory_space=pltpu.HBM)
-    scratch = []
-    if first:
-        source = pltpu.with_memory_space_constraint(source, pltpu.HBM)
-        flat = pltpu.with_memory_space_constraint(flat, pltpu.HBM)
-        scratch = [
-            pltpu.VMEM(shape, jnp.bfloat16),
+    return pl.pallas_call(
+        functools.partial(first_kernel, distances, rest),
+        in_specs=[hbm, hbm],
+        out_specs=[vmem] * 3,
+        out_shape=[
+            jax.ShapeDtypeStruct((depth, count * pixels), jnp.bfloat16),
+            jax.ShapeDtypeStruct((2, len(distances), *stack.shape), jnp.float32),
+            jax.ShapeDtypeStruct((len(rest), depth, 2 * owned), jnp.bfloat16),
+        ],
+        scratch_shapes=[
+            pltpu.VMEM(stack.shape, jnp.bfloat16),
             pltpu.VMEM((len(distances), depth, 2 * owned), jnp.bfloat16),
-            pltpu.SemaphoreType.DMA((1 + len(distances),)),
-        ]
+            pltpu.SemaphoreType.DMA((1 + len(distances) + len(rest),)),
+        ],
+        compiler_params=pltpu.CompilerParams(vmem_limit_bytes=24 * 2**20),
+        cost_estimate=kernel_cost(depth, stack.shape, len(distances)),
+        name="far_partials",
+    )(pltpu.with_memory_space_constraint(stack, pltpu.HBM), pltpu.with_memory_space_constraint(flat, pltpu.HBM))
+
+
+def next_partials(patches, weights, before, after, shape):
+    vmem, unread = pl.BlockSpec(memory_space=pltpu.VMEM), pl.BlockSpec(memory_space=pl.ANY)
     return pl.pallas_call(
-        functools.partial(first_kernel if first else next_kernel, distances),
-        in_specs=[hbm, hbm] if first else [vmem, vmem],
-        out_specs=[vmem] * 2 if first else vmem,
-        out_shape=[patches, sums] if first else sums,
-        scratch_shapes=scratch,
+        next_kernel,
+        in_specs=[vmem, vmem, unread, unread],
+        out_specs=vmem,
+        out_shape=jax.ShapeDtypeStruct((2, weights.shape[0], *shape), jnp.float32),
         compiler_params=pltpu.CompilerParams(vmem_limit_bytes=24 * 2**20),
-        cost_estimate=pl.CostEstimate(
-            flops=4 * depth * len(distances) * owned * count * pixels,
-            bytes_accessed=4 * depth * len(distances) * owned,
-            transcendentals=0,
-        ),
-        name="partials_" + "_".join(map(str, distances)),
-    )(source, flat)
+        cost_estimate=kernel_cost(patches.shape[0], shape, weights.shape[0]),
+        name="near_partials",
+    )(patches, weights, before, after)
 
 
 def conv_halving(stack, flat, layer_bias):
@@ -137,24 +152,36 @@
     def wide(value):
         return value.astype(jnp.float32)
 
-    def core_sums(distances, out):
-        came = swap(out[1].astype(SENT), 1)
-        return {d: [out[0, at, i] + wide(came[at, i]) for i in images] for at, d in enumerate(distances)}
-
-    def across(sums, distance):
-        return swap(jnp.stack([value.astype(SENT) for value in sums]), 2 * distance)
-
-    far, near = (7, 6, 5, 4), (3, 2, 1, 0)
-    patches, out = partials(far, stack, flat, shape, first=True)
-    later = partials(near, patches, flat, shape)
-    sums = core_sums(far, out)
-    came = [across(sums[d], d - 4) for d in (5, 6, 7)]
-    kept = [sums[4][i] + sum(wide(c[i]) for c in came) for i in images]
-    sums = core_sums(near, later)
-    came = [across(sums[d], d) for d in (1, 2, 3)]
-    came.append(across(kept, 4))
+    def core_sums(distances, parts, out):
+        sums = {}
+        for part in parts:
+            first = distances.index(part[0])
+            came = swap(out[1, first : first + len(part)].astype(SENT), 1)
+            for k, d in enumerate(part):
+                sums[d] = [out[0, first + k, i] + wide(came[k, i]) for i in images]
+        return sums
+
+    def across(sums, bit):
+        came = swap(jnp.stack([value.astype(SENT) for value in sums]), 2 * bit)
+        return [wide(came[i]) for i in images]
+
+    def plus(sums, *others):
+        for other in others:
+            sums = [a + b for a, b in zip(sums, other)]
+        return sums
+
+    far, near = (7, 6, 5, 4), (3, 1, 2, 0)
+    patches, out, weights = first_partials(far, near, stack, flat)
+    sums = core_sums(far, (far,), out)
+    near_out = next_partials(patches, weights, out, sums[7][0], shape)
+    sums.update(core_sums(near, ((3,), (1, 2), (0,)), near_out))
+    came5 = across(sums[5], 1)
+    came6 = across(plus(sums[6], across(sums[7], 1)), 2)
+    came4 = across(plus(sums[4], came5, came6), 4)
+    came2 = across(plus(sums[2], across(sums[3], 1)), 2)
+    came1 = across(sums[1], 1)
+    total = plus(sums[0], came4, came2, came1)
     bias = layer_bias[:, None]
-    total = [sums[0][i] + sum(wide(c[i]) for c in came) for i in images]
     return jnp.stack([(wide(stack[i]) + jnp.maximum(total[i] + bias, 0.0)).astype(jnp.bfloat16) for i in images])
 
 

time: 38.4 us -> 35.2 us (0.917)
  waiting for transfers between devices: 14.3 us -> 10.3 us
  starting transfers between devices: 13.5 us -> 14.1 us
    ppermute x9 -> x11, waiting for transfers between devices: 14.3 us -> 10.3 us  [swap(): return lax.ppermute(value, AXIS, [(i, i ^ bits) for i in range(size)])]
    ppermute x9 -> x11, starting transfers between devices: 13.5 us -> 14.1 us  [swap(): return lax.ppermute(value, AXIS, [(i, i ^ bits) for i in range(size)])]
  transfers between devices with their start and end apart: 9 -> 11, of which waited for: 5 -> 5; matrix products, arithmetic and copies ran while one was open for 2% -> 3% of each run, Pallas kernels for 8% -> 9%
where the time goes in v3:
time: 35.2 us; the launch traced here: 35 us
  starting transfers between devices  14.1 us (40%)
  waiting for transfers between devices  10.3 us (29%)
  Pallas kernels  8.19 us (23%)
  other arithmetic  2.1 us (6%)
    ppermute x11, starting transfers between devices, swap(): return lax.ppermute(value, AXIS, [(i, i ^ bits) for i in range(size)])  14.1 us
    ppermute x11, waiting for transfers between devices, swap(): return lax.ppermute(value, AXIS, [(i, i ^ bits) for i in range(size)])  10.3 us
    pallas_call x1, Pallas kernels, first_partials(): pl.pallas_call(functools.partial(first_kernel, distances, rest), in_specs...  5.16 us
    pallas_call x1, Pallas kernels, next_partials(): pl.pallas_call(next_kernel, in_specs=[vmem, vmem, unread, unread], out_sp...  3.03 us
  transfers between devices with their start and end apart: 11, of which 5 were waited for; matrix products, arithmetic and copies ran while one was open for 3% of the time, Pallas kernels for 9%

profile of v3, /device:TPU:0, one launch (start us, length us, event | category | flops | bytes accessed | tf_op | source)
XLA Modules:
  0.0 35.0 jit_solution(3380646500414933837)
XLA Ops:
  0.0 5.2 %far_partials.1 = (bf16[1728,512]{1,0:T(8,128)(2,1)S(1)}, f32[2,4,2,192,256]{4,3,2,1,0:T(8,128)S(1)}, bf16[4,1728,384]{2,1,0:T(8,128)(2,1)S(1)}) custom-call(bf16[2,192,256]{2,1,0:T(8,128)(2,1)} %maps_ref.1, bf16[1728,3072]{1,0:T(8,128)(2,1)} %bitcast.189), custom_call_target="tpu_custom_call" | custom-call | flops 2717908992 | bytes 5308416 | tf_op jit(solution)/shard_map/far_partials/pallas_call | solution.py:111
  5.2 0.1 fusion
  5.3 0.5 %collective-permute-start = (f16[4,2,192,256]{3,2,1,0:T(8,128)(2,1)S(1)}, f16[4,2,192,256]{3,2,1,0:T(8,128)(2,1)S(1)}, u32[]{:S(2)}, u32[]{:S(2)}) collective-permute-start(f16[4,2,192,256]{3,2,1,0:T(8,128)(2,1)S(1)} %fusion), channel_id=1, source_target_pairs={{0,1},{1,0},{2,3},{3,2},{4,5},{5,4},{6,7},{7,6},{8,9},{9,8},{10,11... | collective-permute-start | bytes 2359304 | tf_op jit(solution)/shard_map/ppermute | solution.py:150
  5.8 1.9 %collective-permute-done = f16[4,2,192,256]{3,2,1,0:T(8,128)(2,1)S(1)} collective-permute-done((f16[4,2,192,256]{3,2,1,0:T(8,128)(2,1)S(1)}, f16[4,2,192,256]{3,2,1,0:T(8,128)(2,1)S(1)}, u32[]{:S(2)}, u32[]{:S(2)}) %collective-permute-start) | collective-permute-done | bytes 786464 | tf_op jit(solution)/shard_map/ppermute | solution.py:150
  7.7 0.1 fusion.43
  7.9 3.0 %collective-permute-start.3 = (f16[2,192,256]{2,1,0:T(8,128)(2,1)S(1)}, f16[2,192,256]{2,1,0:T(8,128)(2,1)S(1)}, u32[]{:S(2)}, u32[]{:S(2)}) collective-permute-start(f16[2,192,256]{2,1,0:T(8,128)(2,1)S(1)} %pad_maximum_fusion.1), channel_id=1, source_target_pairs={{0,2},{1,3},{2,0},{3,1},{4,6},{5,7},{6,4},{7,5},{8,10},{9,11},{10,... | collective-permute-start | bytes 589832 | tf_op jit(solution)/shard_map/ppermute | solution.py:150
  10.9 0.1 collective-permute-start.2
  11.0 3.0 %near_partials.1 = f32[2,4,2,192,256]{4,3,2,1,0:T(8,128)S(1)} custom-call(bf16[1728,512]{1,0:T(8,128)(2,1)S(1)} %get-tuple-element.8.x_ref, bf16[4,1728,384]{2,1,0:T(8,128)(2,1)S(1)} %get-tuple-element.9.w_ref, f32[2,4,2,192,256]{4,3,2,1,0:T(8,128)S(1)} %get-tuple-element.10.before_ref, f32[192,256]{1,0:T(8,128)S(1)} %fusion.1.after_ref), custom_call_target="tpu_custom_call" | custom-call | flops 2717908992 | bytes 5308416 | tf_op jit(solution)/shard_map/near_partials/pallas_call | solution.py:133
  14.1 0.3 convert.26
  14.6 0.6 %collective-permute-start.6 = (f16[2,2,192,256]{3,2,1,0:T(8,128)(2,1)S(1)}, f16[2,2,192,256]{3,2,1,0:T(8,128)(2,1)S(1)}, u32[]{:S(2)}, u32[]{:S(2)}) collective-permute-start(f16[2,2,192,256]{3,2,1,0:T(8,128)(2,1)S(1)} %slice_bitcast_fusion), channel_id=1, source_target_pairs={{0,1},{1,0},{2,3},{3,2},{4,5},{5,4},{6,7},{7,6},{8,9},{9,8},{10,11... | collective-permute-start | bytes 1179656 | tf_op jit(solution)/shard_map/ppermute | solution.py:150
  15.1 0.1 collective-permute-start.1
  15.2 1.3 %collective-permute-done.3 = f16[2,192,256]{2,1,0:T(8,128)(2,1)S(1)} collective-permute-done((f16[2,192,256]{2,1,0:T(8,128)(2,1)S(1)}, f16[2,192,256]{2,1,0:T(8,128)(2,1)S(1)}, u32[]{:S(2)}, u32[]{:S(2)}) %collective-permute-start.3) | collective-permute-done | bytes 196640 | tf_op jit(solution)/shard_map/ppermute | solution.py:150
  16.7 2.2 %collective-permute-start.4 = (f16[2,192,256]{2,1,0:T(8,128)(2,1)S(1)}, f16[2,192,256]{2,1,0:T(8,128)(2,1)S(1)}, u32[]{:S(2)}, u32[]{:S(2)}) collective-permute-start(f16[2,192,256]{2,1,0:T(8,128)(2,1)S(1)} %pad_maximum_fusion.2), channel_id=1, source_target_pairs={{0,4},{1,5},{2,6},{3,7},{4,0},{5,1},{6,2},{7,3},{8,12},{9,13},{10,... | collective-permute-start | bytes 589832 | tf_op jit(solution)/shard_map/ppermute | solution.py:150
  19.0 1.6 %collective-permute-start.8 = (f16[2,192,256]{2,1,0:T(8,128)(2,1)S(1)}, f16[2,192,256]{2,1,0:T(8,128)(2,1)S(1)}, u32[]{:S(2)}, u32[]{:S(2)}) collective-permute-start(f16[2,192,256]{2,1,0:T(8,128)(2,1)S(1)} %pad_maximum_fusion.4), channel_id=1, source_target_pairs={{0,2},{1,3},{2,0},{3,1},{4,6},{5,7},{6,4},{7,5},{8,10},{9,11},{10,... | collective-permute-start | bytes 589832 | tf_op jit(solution)/shard_map/ppermute | solution.py:150
  20.6 2.4 %collective-permute-done.4 = f16[2,192,256]{2,1,0:T(8,128)(2,1)S(1)} collective-permute-done((f16[2,192,256]{2,1,0:T(8,128)(2,1)S(1)}, f16[2,192,256]{2,1,0:T(8,128)(2,1)S(1)}, u32[]{:S(2)}, u32[]{:S(2)}) %collective-permute-start.4) | collective-permute-done | bytes 196640 | tf_op jit(solution)/shard_map/ppermute | solution.py:150
  23.0 0.1 fusion.46
  23.1 2.8 %collective-permute-start.5 = (f16[2,192,256]{2,1,0:T(8,128)(2,1)S(1)}, f16[2,192,256]{2,1,0:T(8,128)(2,1)S(1)}, u32[]{:S(2)}, u32[]{:S(2)}) collective-permute-start(f16[2,192,256]{2,1,0:T(8,128)(2,1)S(1)} %pad_maximum_fusion.3), channel_id=1, source_target_pairs={{0,8},{1,9},{2,10},{3,11},{4,12},{5,13},{6,14},{7,15},{8,0},{9,1},... | collective-permute-start | bytes 589832 | tf_op jit(solution)/shard_map/ppermute | solution.py:150
  26.0 0.1 fusion.25
  26.2 1.6 %collective-permute-start.9 = (f16[2,192,256]{2,1,0:T(8,128)(2,1)S(1)}, f16[2,192,256]{2,1,0:T(8,128)(2,1)S(1)}, u32[]{:S(2)}, u32[]{:S(2)}) collective-permute-start(f16[2,192,256]{2,1,0:T(8,128)(2,1)S(1)} %pad_maximum_fusion.5), channel_id=1, source_target_pairs={{0,4},{1,5},{2,6},{3,7},{4,0},{5,1},{6,2},{7,3},{8,12},{9,13},{10,... | collective-permute-start | bytes 589832 | tf_op jit(solution)/shard_map/ppermute | solution.py:150
  27.9 1.6 %collective-permute-start.10 = (f16[2,192,256]{2,1,0:T(8,128)(2,1)S(1)}, f16[2,192,256]{2,1,0:T(8,128)(2,1)S(1)}, u32[]{:S(2)}, u32[]{:S(2)}) collective-permute-start(f16[2,192,256]{2,1,0:T(8,128)(2,1)S(1)} %pad_maximum_fusion.6), channel_id=1, source_target_pairs={{0,2},{1,3},{2,0},{3,1},{4,6},{5,7},{6,4},{7,5},{8,10},{9,11},{10,... | collective-permute-start | bytes 589832 | tf_op jit(solution)/shard_map/ppermute | solution.py:150
  29.4 4.2 %collective-permute-done.5 = f16[2,192,256]{2,1,0:T(8,128)(2,1)S(1)} collective-permute-done((f16[2,192,256]{2,1,0:T(8,128)(2,1)S(1)}, f16[2,192,256]{2,1,0:T(8,128)(2,1)S(1)}, u32[]{:S(2)}, u32[]{:S(2)}) %collective-permute-start.5) | collective-permute-done | bytes 196640 | tf_op jit(solution)/shard_map/ppermute | solution.py:150
  33.6 0.5 %collective-permute-done.9 = f16[2,192,256]{2,1,0:T(8,128)(2,1)S(1)} collective-permute-done((f16[2,192,256]{2,1,0:T(8,128)(2,1)S(1)}, f16[2,192,256]{2,1,0:T(8,128)(2,1)S(1)}, u32[]{:S(2)}, u32[]{:S(2)}) %collective-permute-start.9) | collective-permute-done | bytes 196640 | tf_op jit(solution)/shard_map/ppermute | solution.py:150
  34.1 0.2 fusion.33
  34.3 0.7 %pad_maximum_fusion.7 = bf16[2,192,256]{2,1,0:T(8,128)(2,1)} fusion(bf16[1,192,256]{2,1,0:T(8,128)(2,1)S(1)} %get-tuple-element.14, bf16[1,192,256]{2,1,0:T(8,128)(2,1)S(1)} %get-tuple-element.13), kind=kLoop, calls=%fused_computation.55 | loop fusion | flops 98304 | bytes 393216 | tf_op jit(solution)/shard_map/stack | solution.py:185
  (23 shorter events, 0.8 us)
Async XLA Ops:
  5.3 2.4 %collective-permute-start = (f16[4,2,192,256]{3,2,1,0:T(8,128)(2,1)S(1)}, f16[4,2,192,256]{3,2,1,0:T(8,128)(2,1)S(1)}, u32[]{:S(2)}, u32[]{:S(2)}) collective-permute-start(f16[4,2,192,256]{3,2,1,0:T(8,128)(2,1)S(1)} %fusion), channel_id=1, source_target_pairs={{0,1},{1,0},{2,3},{3,2},{4,5},{5,4},{6,7},{7,6},{8,9},{9,8},{10,11... | collective-permute-start | bytes 2359304 | tf_op jit(solution)/shard_map/ppermute | solution.py:150
  7.9 8.6 %collective-permute-start.3 = (f16[2,192,256]{2,1,0:T(8,128)(2,1)S(1)}, f16[2,192,256]{2,1,0:T(8,128)(2,1)S(1)}, u32[]{:S(2)}, u32[]{:S(2)}) collective-permute-start(f16[2,192,256]{2,1,0:T(8,128)(2,1)S(1)} %pad_maximum_fusion.1), channel_id=1, source_target_pairs={{0,2},{1,3},{2,0},{3,1},{4,6},{5,7},{6,4},{7,5},{8,10},{9,11},{10,... | collective-permute-start | bytes 589832 | tf_op jit(solution)/shard_map/ppermute | solution.py:150
  10.9 9.7 %collective-permute-start.2 = (f16[2,192,256]{2,1,0:T(8,128)(2,1)S(1)}, f16[2,192,256]{2,1,0:T(8,128)(2,1)S(1)}, u32[]{:S(2)}, u32[]{:S(2)}) collective-permute-start(f16[2,192,256]{2,1,0:T(8,128)(2,1)S(1)} %pad_maximum_fusion), channel_id=1, source_target_pairs={{0,2},{1,3},{2,0},{3,1},{4,6},{5,7},{6,4},{7,5},{8,10},{9,11},{10,... | collective-permute-start | bytes 589832 | tf_op jit(solution)/shard_map/ppermute | solution.py:150
  14.4 4.4 %collective-permute-start.7 = (f16[1,2,192,256]{3,2,1,0:T(8,128)(2,1)S(1)}, f16[1,2,192,256]{3,2,1,0:T(8,128)(2,1)S(1)}, u32[]{:S(2)}, u32[]{:S(2)}) collective-permute-start(f16[1,2,192,256]{3,2,1,0:T(8,128)(2,1)S(1)} %get-tuple-element.28), channel_id=1, source_target_pairs={{0,1},{1,0},{2,3},{3,2},{4,5},{5,4},{6,7},{7,6},{8,9},{9,8},{10,11... | collective-permute-start | bytes 589832 | tf_op jit(solution)/shard_map/ppermute | solution.py:150
  14.6 11.4 %collective-permute-start.6 = (f16[2,2,192,256]{3,2,1,0:T(8,128)(2,1)S(1)}, f16[2,2,192,256]{3,2,1,0:T(8,128)(2,1)S(1)}, u32[]{:S(2)}, u32[]{:S(2)}) collective-permute-start(f16[2,2,192,256]{3,2,1,0:T(8,128)(2,1)S(1)} %slice_bitcast_fusion), channel_id=1, source_target_pairs={{0,1},{1,0},{2,3},{3,2},{4,5},{5,4},{6,7},{7,6},{8,9},{9,8},{10,11... | collective-permute-start | bytes 1179656 | tf_op jit(solution)/shard_map/ppermute | solution.py:150
  15.1 19.0 %copy-start = (bf16[2,192,256]{2,1,0:T(8,128)(2,1)S(1)}, bf16[2,192,256]{2,1,0:T(8,128)(2,1)}, u32[]{:S(2)}) copy-start(bf16[2,192,256]{2,1,0:T(8,128)(2,1)} %maps_ref.1) | copy-start | bytes 589828
  15.1 19.0 %copy-start.1 = (f32[1,192]{1,0:T(1,128)S(1)}, f32[1,192]{1,0:T(1,128)}, u32[]{:S(2)}) copy-start(f32[1,192]{1,0:T(1,128)} %param.5) | copy-start | bytes 2308
  15.1 14.3 %collective-permute-start.1 = (f16[1,2,192,256]{3,2,1,0:T(8,128)(2,1)S(1)}, f16[1,2,192,256]{3,2,1,0:T(8,128)(2,1)S(1)}, u32[]{:S(2)}, u32[]{:S(2)}) collective-permute-start(f16[1,2,192,256]{3,2,1,0:T(8,128)(2,1)S(1)} %get-tuple-element.27), channel_id=1, source_target_pairs={{0,1},{1,0},{2,3},{3,2},{4,5},{5,4},{6,7},{7,6},{8,9},{9,8},{10,11... | collective-permute-start | bytes 589832 | tf_op jit(solution)/shard_map/ppermute | solution.py:150
  16.7 6.3 %collective-permute-start.4 = (f16[2,192,256]{2,1,0:T(8,128)(2,1)S(1)}, f16[2,192,256]{2,1,0:T(8,128)(2,1)S(1)}, u32[]{:S(2)}, u32[]{:S(2)}) collective-permute-start(f16[2,192,256]{2,1,0:T(8,128)(2,1)S(1)} %pad_maximum_fusion.2), channel_id=1, source_target_pairs={{0,4},{1,5},{2,6},{3,7},{4,0},{5,1},{6,2},{7,3},{8,12},{9,13},{10,... | collective-permute-start | bytes 589832 | tf_op jit(solution)/shard_map/ppermute | solution.py:150
  19.0 7.0 %collective-permute-start.8 = (f16[2,192,256]{2,1,0:T(8,128)(2,1)S(1)}, f16[2,192,256]{2,1,0:T(8,128)(2,1)S(1)}, u32[]{:S(2)}, u32[]{:S(2)}) collective-permute-start(f16[2,192,256]{2,1,0:T(8,128)(2,1)S(1)} %pad_maximum_fusion.4), channel_id=1, source_target_pairs={{0,2},{1,3},{2,0},{3,1},{4,6},{5,7},{6,4},{7,5},{8,10},{9,11},{10,... | collective-permute-start | bytes 589832 | tf_op jit(solution)/shard_map/ppermute | solution.py:150
  23.1 10.5 %collective-permute-start.5 = (f16[2,192,256]{2,1,0:T(8,128)(2,1)S(1)}, f16[2,192,256]{2,1,0:T(8,128)(2,1)S(1)}, u32[]{:S(2)}, u32[]{:S(2)}) collective-permute-start(f16[2,192,256]{2,1,0:T(8,128)(2,1)S(1)} %pad_maximum_fusion.3), channel_id=1, source_target_pairs={{0,8},{1,9},{2,10},{3,11},{4,12},{5,13},{6,14},{7,15},{8,0},{9,1},... | collective-permute-start | bytes 589832 | tf_op jit(solution)/shard_map/ppermute | solution.py:150
  26.2 8.0 %collective-permute-start.9 = (f16[2,192,256]{2,1,0:T(8,128)(2,1)S(1)}, f16[2,192,256]{2,1,0:T(8,128)(2,1)S(1)}, u32[]{:S(2)}, u32[]{:S(2)}) collective-permute-start(f16[2,192,256]{2,1,0:T(8,128)(2,1)S(1)} %pad_maximum_fusion.5), channel_id=1, source_target_pairs={{0,4},{1,5},{2,6},{3,7},{4,0},{5,1},{6,2},{7,3},{8,12},{9,13},{10,... | collective-permute-start | bytes 589832 | tf_op jit(solution)/shard_map/ppermute | solution.py:150
  27.9 6.3 %collective-permute-start.10 = (f16[2,192,256]{2,1,0:T(8,128)(2,1)S(1)}, f16[2,192,256]{2,1,0:T(8,128)(2,1)S(1)}, u32[]{:S(2)}, u32[]{:S(2)}) collective-permute-start(f16[2,192,256]{2,1,0:T(8,128)(2,1)S(1)} %pad_maximum_fusion.6), channel_id=1, source_target_pairs={{0,2},{1,3},{2,0},{3,1},{4,6},{5,7},{6,4},{7,5},{8,10},{9,11},{10,... | collective-permute-start | bytes 589832 | tf_op jit(solution)/shard_map/ppermute | solution.py:150

commit v4 on v3

--- a/solution.py
+++ b/solution.py
@@ -91,10 +91,11 @@
         copy.wait()
 
 
-def next_kernel(x_ref, w_ref, before_ref, after_ref, out_ref):
+def next_kernel(first, x_ref, w_ref, *refs):
+    out_ref = refs[-1]
     low = lax.rem(lax.axis_index(AXIS), 2)
-    for at in range(w_ref.shape[0]):
-        contribution(x_ref, w_ref[at], low, out_ref.at[:, at])
+    for at in range(out_ref.shape[1]):
+        contribution(x_ref, w_ref[first + at], low, out_ref.at[:, at])
 
 
 def kernel_cost(depth, shape, chunks):
@@ -124,21 +125,21 @@
         ],
         compiler_params=pltpu.CompilerParams(vmem_limit_bytes=24 * 2**20),
         cost_estimate=kernel_cost(depth, stack.shape, len(distances)),
-        name="far_partials",
+        name="partials_and_patches",
     )(pltpu.with_memory_space_constraint(stack, pltpu.HBM), pltpu.with_memory_space_constraint(flat, pltpu.HBM))
 
 
-def next_partials(patches, weights, before, after, shape):
+def next_partials(patches, weights, first, chunks, shape, before):
     vmem, unread = pl.BlockSpec(memory_space=pltpu.VMEM), pl.BlockSpec(memory_space=pl.ANY)
     return pl.pallas_call(
-        next_kernel,
-        in_specs=[vmem, vmem, unread, unread],
+        functools.partial(next_kernel, first),
+        in_specs=[vmem, vmem] + [unread] * len(before),
         out_specs=vmem,
-        out_shape=jax.ShapeDtypeStruct((2, weights.shape[0], *shape), jnp.float32),
+        out_shape=jax.ShapeDtypeStruct((2, chunks, *shape), jnp.float32),
         compiler_params=pltpu.CompilerParams(vmem_limit_bytes=24 * 2**20),
-        cost_estimate=kernel_cost(patches.shape[0], shape, weights.shape[0]),
-        name="near_partials",
-    )(patches, weights, before, after)
+        cost_estimate=kernel_cost(patches.shape[0], shape, chunks),
+        name="partials_" + str(first),
+    )(patches, weights, *before)
 
 
 def conv_halving(stack, flat, layer_bias):
@@ -170,10 +171,12 @@
             sums = [a + b for a, b in zip(sums, other)]
         return sums
 
-    far, near = (7, 6, 5, 4), (3, 1, 2, 0)
-    patches, out, weights = first_partials(far, near, stack, flat)
-    sums = core_sums(far, (far,), out)
-    near_out = next_partials(patches, weights, out, sums[7][0], shape)
+    odd, even, near = (7, 5), (6, 4), (3, 1, 2, 0)
+    patches, odd_out, weights = first_partials(odd, even + near, stack, flat)
+    even_out = next_partials(patches, weights, 0, len(even), shape, (odd_out,))
+    sums = core_sums(odd, (odd,), odd_out)
+    sums.update(core_sums(even, (even,), even_out))
+    near_out = next_partials(patches, weights, len(even), len(near), shape, (even_out, sums[7][0]))
     sums.update(core_sums(near, ((3,), (1, 2), (0,)), near_out))
     came5 = across(sums[5], 1)
     came6 = across(plus(sums[6], across(sums[7], 1)), 2)

time: 35.2 us -> 34.2 us (0.972)
  waiting for transfers between devices: 10.3 us -> 8.37 us
  Pallas kernels: 8.19 us -> 8.97 us
    ppermute x11 -> x12, waiting for transfers between devices: 10.3 us -> 8.37 us  [swap(): return lax.ppermute(value, AXIS, [(i, i ^ bits) for i in range(size)])]
    pallas_call x1 -> x2, Pallas kernels: 3.03 us -> 4.64 us  [next_partials(): pl.pallas_call(functools.partial(next_kernel, first), in_specs=[vmem, vme...]
    pallas_call x1, Pallas kernels: 5.16 us -> 4.34 us  [first_partials(): pl.pallas_call(functools.partial(first_kernel, distances, rest), in_specs...]
    ppermute x11 -> x12, starting transfers between devices: 14.1 us -> 14.3 us  [swap(): return lax.ppermute(value, AXIS, [(i, i ^ bits) for i in range(size)])]
  transfers between devices with their start and end apart: 11 -> 12, of which waited for: 5 -> 4; matrix products, arithmetic and copies ran while one was open for 3% -> 4% of each run, Pallas kernels for 9% -> 14%
where the time goes in v4:
time: 34.2 us; the launch traced here: 34.1 us
  starting transfers between devices  14.3 us (42%)
  Pallas kernels  8.97 us (26%)
  waiting for transfers between devices  8.37 us (24%)
  other arithmetic  2.09 us (6%)
    ppermute x12, starting transfers between devices, swap(): return lax.ppermute(value, AXIS, [(i, i ^ bits) for i in range(size)])  14.3 us
    ppermute x12, waiting for transfers between devices, swap(): return lax.ppermute(value, AXIS, [(i, i ^ bits) for i in range(size)])  8.37 us
    pallas_call x2, Pallas kernels, next_partials(): pl.pallas_call(functools.partial(next_kernel, first), in_specs=[vmem, vme...  4.64 us
    pallas_call x1, Pallas kernels, first_partials(): pl.pallas_call(functools.partial(first_kernel, distances, rest), in_specs...  4.34 us
    another operation x1, other arithmetic, conv_halving(): jnp.stack([(wide(stack[i]) + jnp.maximum(total[i] + bias, 0.0)).astype(jn...  0.7 us
  transfers between devices with their start and end apart: 12, of which 4 were waited for; matrix products, arithmetic and copies ran while one was open for 4% of the time, Pallas kernels for 14%

profile of v4, /device:TPU:0, one launch (start us, length us, event | category | flops | bytes accessed | tf_op | source)
XLA Modules:
  0.0 34.1 jit_solution(295322956683376017)
XLA Ops:
  0.0 4.3 %partials_and_patches.1 = (bf16[1728,512]{1,0:T(8,128)(2,1)S(1)}, f32[2,2,2,192,256]{4,3,2,1,0:T(8,128)S(1)}, bf16[6,1728,384]{2,1,0:T(8,128)(2,1)S(1)}) custom-call(bf16[2,192,256]{2,1,0:T(8,128)(2,1)} %maps_ref.1, bf16[1728,3072]{1,0:T(8,128)(2,1)} %bitcast.219), custom_call_target="tpu_custom_call" | custom-call | flops 1358954496 | bytes 2654208 | tf_op jit(solution)/shard_map/partials_and_patches/pallas_call | solution.py:112
  4.4 0.5 %collective-permute-start = (f16[2,2,192,256]{3,2,1,0:T(8,128)(2,1)S(1)}, f16[2,2,192,256]{3,2,1,0:T(8,128)(2,1)S(1)}, u32[]{:S(2)}, u32[]{:S(2)}) collective-permute-start(f16[2,2,192,256]{3,2,1,0:T(8,128)(2,1)S(1)} %fusion), channel_id=1, source_target_pairs={{0,1},{1,0},{2,3},{3,2},{4,5},{5,4},{6,7},{7,6},{8,9},{9,8},{10,11... | collective-permute-start | bytes 1179656 | tf_op jit(solution)/shard_map/ppermute | solution.py:151
  4.9 1.6 %partials_0.1.refs_0_ = f32[2,2,2,192,256]{4,3,2,1,0:T(8,128)S(1)} custom-call(bf16[1728,512]{1,0:T(8,128)(2,1)S(1)} %get-tuple-element.8.x_ref, bf16[6,1728,384]{2,1,0:T(8,128)(2,1)S(1)} %get-tuple-element.9.w_ref, f32[2,2,2,192,256]{4,3,2,1,0:T(8,128)S(1)} %get-tuple-element.10.refs_0_), custom_call_target="tpu_custom_call" | custom-call | flops 1358954496 | bytes 2654208 | tf_op jit(solution)/shard_map/partials_0/pallas_call | solution.py:134
  6.6 0.1 collective-permute-start.2
  6.7 0.1 fusion.51
  6.9 3.0 %collective-permute-start.4 = (f16[2,192,256]{2,1,0:T(8,128)(2,1)S(1)}, f16[2,192,256]{2,1,0:T(8,128)(2,1)S(1)}, u32[]{:S(2)}, u32[]{:S(2)}) collective-permute-start(f16[2,192,256]{2,1,0:T(8,128)(2,1)S(1)} %pad_maximum_fusion.1), channel_id=1, source_target_pairs={{0,2},{1,3},{2,0},{3,1},{4,6},{5,7},{6,4},{7,5},{8,10},{9,11},{10,... | collective-permute-start | bytes 589832 | tf_op jit(solution)/shard_map/ppermute | solution.py:151
  10.0 0.1 collective-permute-start.3
  10.1 3.0 %partials_2.1 = f32[2,4,2,192,256]{4,3,2,1,0:T(8,128)S(1)} custom-call(bf16[1728,512]{1,0:T(8,128)(2,1)S(1)} %get-tuple-element.8.x_ref, bf16[6,1728,384]{2,1,0:T(8,128)(2,1)S(1)} %get-tuple-element.9.w_ref, f32[2,2,2,192,256]{4,3,2,1,0:T(8,128)S(1)} %partials_0.1.refs_0_, f32[192,256]{1,0:T(8,128)S(1)} %fusion.2.refs_1_), custom_call_target="tpu_custom_call" | custom-call | flops 2717908992 | bytes 5308416 | tf_op jit(solution)/shard_map/partials_2/pallas_call | solution.py:134
  13.1 0.3 convert.29
  13.7 0.6 %collective-permute-start.7 = (f16[2,2,192,256]{3,2,1,0:T(8,128)(2,1)S(1)}, f16[2,2,192,256]{3,2,1,0:T(8,128)(2,1)S(1)}, u32[]{:S(2)}, u32[]{:S(2)}) collective-permute-start(f16[2,2,192,256]{3,2,1,0:T(8,128)(2,1)S(1)} %slice_bitcast_fusion), channel_id=1, source_target_pairs={{0,1},{1,0},{2,3},{3,2},{4,5},{5,4},{6,7},{7,6},{8,9},{9,8},{10,11... | collective-permute-start | bytes 1179656 | tf_op jit(solution)/shard_map/ppermute | solution.py:151
  14.2 0.1 collective-permute-start.1
  14.3 1.3 %collective-permute-done.4 = f16[2,192,256]{2,1,0:T(8,128)(2,1)S(1)} collective-permute-done((f16[2,192,256]{2,1,0:T(8,128)(2,1)S(1)}, f16[2,192,256]{2,1,0:T(8,128)(2,1)S(1)}, u32[]{:S(2)}, u32[]{:S(2)}) %collective-permute-start.4) | collective-permute-done | bytes 196640 | tf_op jit(solution)/shard_map/ppermute | solution.py:151
  15.8 2.2 %collective-permute-start.5 = (f16[2,192,256]{2,1,0:T(8,128)(2,1)S(1)}, f16[2,192,256]{2,1,0:T(8,128)(2,1)S(1)}, u32[]{:S(2)}, u32[]{:S(2)}) collective-permute-start(f16[2,192,256]{2,1,0:T(8,128)(2,1)S(1)} %pad_maximum_fusion.2), channel_id=1, source_target_pairs={{0,4},{1,5},{2,6},{3,7},{4,0},{5,1},{6,2},{7,3},{8,12},{9,13},{10,... | collective-permute-start | bytes 589832 | tf_op jit(solution)/shard_map/ppermute | solution.py:151
  18.1 1.6 %collective-permute-start.9 = (f16[2,192,256]{2,1,0:T(8,128)(2,1)S(1)}, f16[2,192,256]{2,1,0:T(8,128)(2,1)S(1)}, u32[]{:S(2)}, u32[]{:S(2)}) collective-permute-start(f16[2,192,256]{2,1,0:T(8,128)(2,1)S(1)} %pad_maximum_fusion.4), channel_id=1, source_target_pairs={{0,2},{1,3},{2,0},{3,1},{4,6},{5,7},{6,4},{7,5},{8,10},{9,11},{10,... | collective-permute-start | bytes 589832 | tf_op jit(solution)/shard_map/ppermute | solution.py:151
  19.7 2.4 %collective-permute-done.5 = f16[2,192,256]{2,1,0:T(8,128)(2,1)S(1)} collective-permute-done((f16[2,192,256]{2,1,0:T(8,128)(2,1)S(1)}, f16[2,192,256]{2,1,0:T(8,128)(2,1)S(1)}, u32[]{:S(2)}, u32[]{:S(2)}) %collective-permute-start.5) | collective-permute-done | bytes 196640 | tf_op jit(solution)/shard_map/ppermute | solution.py:151
  22.1 0.1 fusion.40
  22.3 2.8 %collective-permute-start.6 = (f16[2,192,256]{2,1,0:T(8,128)(2,1)S(1)}, f16[2,192,256]{2,1,0:T(8,128)(2,1)S(1)}, u32[]{:S(2)}, u32[]{:S(2)}) collective-permute-start(f16[2,192,256]{2,1,0:T(8,128)(2,1)S(1)} %pad_maximum_fusion.3), channel_id=1, source_target_pairs={{0,8},{1,9},{2,10},{3,11},{4,12},{5,13},{6,14},{7,15},{8,0},{9,1},... | collective-permute-start | bytes 589832 | tf_op jit(solution)/shard_map/ppermute | solution.py:151
  25.1 0.1 fusion.26
  25.3 1.6 %collective-permute-start.10 = (f16[2,192,256]{2,1,0:T(8,128)(2,1)S(1)}, f16[2,192,256]{2,1,0:T(8,128)(2,1)S(1)}, u32[]{:S(2)}, u32[]{:S(2)}) collective-permute-start(f16[2,192,256]{2,1,0:T(8,128)(2,1)S(1)} %pad_maximum_fusion.5), channel_id=1, source_target_pairs={{0,4},{1,5},{2,6},{3,7},{4,0},{5,1},{6,2},{7,3},{8,12},{9,13},{10,... | collective-permute-start | bytes 589832 | tf_op jit(solution)/shard_map/ppermute | solution.py:151
  27.0 1.6 %collective-permute-start.11 = (f16[2,192,256]{2,1,0:T(8,128)(2,1)S(1)}, f16[2,192,256]{2,1,0:T(8,128)(2,1)S(1)}, u32[]{:S(2)}, u32[]{:S(2)}) collective-permute-start(f16[2,192,256]{2,1,0:T(8,128)(2,1)S(1)} %pad_maximum_fusion.6), channel_id=1, source_target_pairs={{0,2},{1,3},{2,0},{3,1},{4,6},{5,7},{6,4},{7,5},{8,10},{9,11},{10,... | collective-permute-start | bytes 589832 | tf_op jit(solution)/shard_map/ppermute | solution.py:151
  28.6 4.2 %collective-permute-done.6 = f16[2,192,256]{2,1,0:T(8,128)(2,1)S(1)} collective-permute-done((f16[2,192,256]{2,1,0:T(8,128)(2,1)S(1)}, f16[2,192,256]{2,1,0:T(8,128)(2,1)S(1)}, u32[]{:S(2)}, u32[]{:S(2)}) %collective-permute-start.6) | collective-permute-done | bytes 196640 | tf_op jit(solution)/shard_map/ppermute | solution.py:151
  32.8 0.4 %collective-permute-done.10 = f16[2,192,256]{2,1,0:T(8,128)(2,1)S(1)} collective-permute-done((f16[2,192,256]{2,1,0:T(8,128)(2,1)S(1)}, f16[2,192,256]{2,1,0:T(8,128)(2,1)S(1)}, u32[]{:S(2)}, u32[]{:S(2)}) %collective-permute-start.10) | collective-permute-done | bytes 196640 | tf_op jit(solution)/shard_map/ppermute | solution.py:151
  33.2 0.2 fusion.48
  33.4 0.7 %pad_maximum_fusion.7 = bf16[2,192,256]{2,1,0:T(8,128)(2,1)} fusion(bf16[1,192,256]{2,1,0:T(8,128)(2,1)S(1)} %get-tuple-element.12, bf16[1,192,256]{2,1,0:T(8,128)(2,1)S(1)} %get-tuple-element.11), kind=kLoop, calls=%fused_computation.75 | loop fusion | flops 98304 | bytes 393216 | tf_op jit(solution)/shard_map/stack | solution.py:188
  (27 shorter events, 0.9 us)
Async XLA Ops:
  4.4 2.3 %collective-permute-start = (f16[2,2,192,256]{3,2,1,0:T(8,128)(2,1)S(1)}, f16[2,2,192,256]{3,2,1,0:T(8,128)(2,1)S(1)}, u32[]{:S(2)}, u32[]{:S(2)}) collective-permute-start(f16[2,2,192,256]{3,2,1,0:T(8,128)(2,1)S(1)} %fusion), channel_id=1, source_target_pairs={{0,1},{1,0},{2,3},{3,2},{4,5},{5,4},{6,7},{7,6},{8,9},{9,8},{10,11... | collective-permute-start | bytes 1179656 | tf_op jit(solution)/shard_map/ppermute | solution.py:151
  6.6 7.6 %collective-permute-start.2 = (f16[2,2,192,256]{3,2,1,0:T(8,128)(2,1)S(1)}, f16[2,2,192,256]{3,2,1,0:T(8,128)(2,1)S(1)}, u32[]{:S(2)}, u32[]{:S(2)}) collective-permute-start(f16[2,2,192,256]{3,2,1,0:T(8,128)(2,1)S(1)} %fusion.1), channel_id=1, source_target_pairs={{0,1},{1,0},{2,3},{3,2},{4,5},{5,4},{6,7},{7,6},{8,9},{9,8},{10,11... | collective-permute-start | bytes 1179656 | tf_op jit(solution)/shard_map/ppermute | solution.py:151
  6.9 8.7 %collective-permute-start.4 = (f16[2,192,256]{2,1,0:T(8,128)(2,1)S(1)}, f16[2,192,256]{2,1,0:T(8,128)(2,1)S(1)}, u32[]{:S(2)}, u32[]{:S(2)}) collective-permute-start(f16[2,192,256]{2,1,0:T(8,128)(2,1)S(1)} %pad_maximum_fusion.1), channel_id=1, source_target_pairs={{0,2},{1,3},{2,0},{3,1},{4,6},{5,7},{6,4},{7,5},{8,10},{9,11},{10,... | collective-permute-start | bytes 589832 | tf_op jit(solution)/shard_map/ppermute | solution.py:151
  10.0 9.7 %collective-permute-start.3 = (f16[2,192,256]{2,1,0:T(8,128)(2,1)S(1)}, f16[2,192,256]{2,1,0:T(8,128)(2,1)S(1)}, u32[]{:S(2)}, u32[]{:S(2)}) collective-permute-start(f16[2,192,256]{2,1,0:T(8,128)(2,1)S(1)} %pad_maximum_fusion), channel_id=1, source_target_pairs={{0,2},{1,3},{2,0},{3,1},{4,6},{5,7},{6,4},{7,5},{8,10},{9,11},{10,... | collective-permute-start | bytes 589832 | tf_op jit(solution)/shard_map/ppermute | solution.py:151
  13.5 4.5 %collective-permute-start.8 = (f16[1,2,192,256]{3,2,1,0:T(8,128)(2,1)S(1)}, f16[1,2,192,256]{3,2,1,0:T(8,128)(2,1)S(1)}, u32[]{:S(2)}, u32[]{:S(2)}) collective-permute-start(f16[1,2,192,256]{3,2,1,0:T(8,128)(2,1)S(1)} %get-tuple-element.28), channel_id=1, source_target_pairs={{0,1},{1,0},{2,3},{3,2},{4,5},{5,4},{6,7},{7,6},{8,9},{9,8},{10,11... | collective-permute-start | bytes 589832 | tf_op jit(solution)/shard_map/ppermute | solution.py:151
  13.7 11.4 %collective-permute-start.7 = (f16[2,2,192,256]{3,2,1,0:T(8,128)(2,1)S(1)}, f16[2,2,192,256]{3,2,1,0:T(8,128)(2,1)S(1)}, u32[]{:S(2)}, u32[]{:S(2)}) collective-permute-start(f16[2,2,192,256]{3,2,1,0:T(8,128)(2,1)S(1)} %slice_bitcast_fusion), channel_id=1, source_target_pairs={{0,1},{1,0},{2,3},{3,2},{4,5},{5,4},{6,7},{7,6},{8,9},{9,8},{10,11... | collective-permute-start | bytes 1179656 | tf_op jit(solution)/shard_map/ppermute | solution.py:151
  14.2 14.3 %collective-permute-start.1 = (f16[1,2,192,256]{3,2,1,0:T(8,128)(2,1)S(1)}, f16[1,2,192,256]{3,2,1,0:T(8,128)(2,1)S(1)}, u32[]{:S(2)}, u32[]{:S(2)}) collective-permute-start(f16[1,2,192,256]{3,2,1,0:T(8,128)(2,1)S(1)} %get-tuple-element.27), channel_id=1, source_target_pairs={{0,1},{1,0},{2,3},{3,2},{4,5},{5,4},{6,7},{7,6},{8,9},{9,8},{10,11... | collective-permute-start | bytes 589832 | tf_op jit(solution)/shard_map/ppermute | solution.py:151
  15.8 6.3 %collective-permute-start.5 = (f16[2,192,256]{2,1,0:T(8,128)(2,1)S(1)}, f16[2,192,256]{2,1,0:T(8,128)(2,1)S(1)}, u32[]{:S(2)}, u32[]{:S(2)}) collective-permute-start(f16[2,192,256]{2,1,0:T(8,128)(2,1)S(1)} %pad_maximum_fusion.2), channel_id=1, source_target_pairs={{0,4},{1,5},{2,6},{3,7},{4,0},{5,1},{6,2},{7,3},{8,12},{9,13},{10,... | collective-permute-start | bytes 589832 | tf_op jit(solution)/shard_map/ppermute | solution.py:151
  18.1 7.0 %collective-permute-start.9 = (f16[2,192,256]{2,1,0:T(8,128)(2,1)S(1)}, f16[2,192,256]{2,1,0:T(8,128)(2,1)S(1)}, u32[]{:S(2)}, u32[]{:S(2)}) collective-permute-start(f16[2,192,256]{2,1,0:T(8,128)(2,1)S(1)} %pad_maximum_fusion.4), channel_id=1, source_target_pairs={{0,2},{1,3},{2,0},{3,1},{4,6},{5,7},{6,4},{7,5},{8,10},{9,11},{10,... | collective-permute-start | bytes 589832 | tf_op jit(solution)/shard_map/ppermute | solution.py:151
  22.2 11.0 %copy-start = (bf16[2,192,256]{2,1,0:T(8,128)(2,1)S(1)}, bf16[2,192,256]{2,1,0:T(8,128)(2,1)}, u32[]{:S(2)}) copy-start(bf16[2,192,256]{2,1,0:T(8,128)(2,1)} %maps_ref.1) | copy-start | bytes 589828
  22.2 11.0 %copy-start.1 = (f32[1,192]{1,0:T(1,128)S(1)}, f32[1,192]{1,0:T(1,128)}, u32[]{:S(2)}) copy-start(f32[1,192]{1,0:T(1,128)} %param.5) | copy-start | bytes 2308
  22.3 10.5 %collective-permute-start.6 = (f16[2,192,256]{2,1,0:T(8,128)(2,1)S(1)}, f16[2,192,256]{2,1,0:T(8,128)(2,1)S(1)}, u32[]{:S(2)}, u32[]{:S(2)}) collective-permute-start(f16[2,192,256]{2,1,0:T(8,128)(2,1)S(1)} %pad_maximum_fusion.3), channel_id=1, source_target_pairs={{0,8},{1,9},{2,10},{3,11},{4,12},{5,13},{6,14},{7,15},{8,0},{9,1},... | collective-permute-start | bytes 589832 | tf_op jit(solution)/shard_map/ppermute | solution.py:151
  25.3 7.9 %collective-permute-start.10 = (f16[2,192,256]{2,1,0:T(8,128)(2,1)S(1)}, f16[2,192,256]{2,1,0:T(8,128)(2,1)S(1)}, u32[]{:S(2)}, u32[]{:S(2)}) collective-permute-start(f16[2,192,256]{2,1,0:T(8,128)(2,1)S(1)} %pad_maximum_fusion.5), channel_id=1, source_target_pairs={{0,4},{1,5},{2,6},{3,7},{4,0},{5,1},{6,2},{7,3},{8,12},{9,13},{10,... | collective-permute-start | bytes 589832 | tf_op jit(solution)/shard_map/ppermute | solution.py:151
  27.0 6.2 %collective-permute-start.11 = (f16[2,192,256]{2,1,0:T(8,128)(2,1)S(1)}, f16[2,192,256]{2,1,0:T(8,128)(2,1)S(1)}, u32[]{:S(2)}, u32[]{:S(2)}) collective-permute-start(f16[2,192,256]{2,1,0:T(8,128)(2,1)S(1)} %pad_maximum_fusion.6), channel_id=1, source_target_pairs={{0,2},{1,3},{2,0},{3,1},{4,6},{5,7},{6,4},{7,5},{8,10},{9,11},{10,... | collective-permute-start | bytes 589832 | tf_op jit(solution)/shard_map/ppermute | solution.py:151

commit v5 on v4

--- a/solution.py
+++ b/solution.py
@@ -67,35 +67,37 @@
             out_ref[low ^ core, image] = part[rows, at]
 
 
-def columns_of(distance, width):
+def weights_of(w_ref, distance, width):
     pair = lax.div(lax.axis_index(AXIS), 2)
-    return pl.ds(pl.multiple_of((pair ^ distance) * width, 128), width)
+    start = pl.multiple_of(lax.rem(pair ^ distance, 2) * width, 128)
+    return w_ref[w_ref.shape[0] - 1 - distance // 2, :, pl.ds(start, width)]
 
 
-def first_kernel(distances, rest, maps_ref, w_ref, x_ref, out_ref, rest_ref, maps_buf, w_buf, sems):
-    low = lax.rem(lax.axis_index(AXIS), 2)
-    maps_copy = pltpu.make_async_copy(maps_ref, maps_buf, sems.at[0])
+def first_kernel(distances, maps_ref, flat_ref, x_ref, out_ref, w_ref, maps_buf, sems):
+    me = lax.axis_index(AXIS)
+    low, block = lax.rem(me, 2), lax.div(me, 4)
+    maps_copy = pltpu.make_async_copy(maps_ref, maps_buf, sems.at[w_ref.shape[0]])
     maps_copy.start()
+    width = w_ref.shape[2]
     copies = []
-    for at, distance in enumerate(distances + rest):
-        columns = columns_of(distance, w_buf.shape[2])
-        target = w_buf.at[at] if at < len(distances) else rest_ref.at[at - len(distances)]
-        copies.append(pltpu.make_async_copy(w_ref.at[:, columns], target, sems.at[1 + at]))
+    for at in range(w_ref.shape[0]):
+        start = pl.multiple_of((block ^ (w_ref.shape[0] - 1 - at)) * width, 128)
+        copies.append(pltpu.make_async_copy(flat_ref.at[:, pl.ds(start, width)], w_ref.at[at], sems.at[at]))
         copies[-1].start()
     maps_copy.wait()
     write_patches(maps_buf, x_ref)
-    for at, copy in enumerate(copies[: len(distances)]):
-        copy.wait()
-        contribution(x_ref, w_buf[at], low, out_ref.at[:, at])
+    for at, distance in enumerate(distances):
+        copies[at].wait()
+        contribution(x_ref, weights_of(w_ref, distance, width // 2), low, out_ref.at[:, at])
     for copy in copies[len(distances) :]:
         copy.wait()
 
 
-def next_kernel(first, x_ref, w_ref, *refs):
+def next_kernel(distances, x_ref, w_ref, *refs):
     out_ref = refs[-1]
     low = lax.rem(lax.axis_index(AXIS), 2)
-    for at in range(out_ref.shape[1]):
-        contribution(x_ref, w_ref[first + at], low, out_ref.at[:, at])
+    for at, distance in enumerate(distances):
+        contribution(x_ref, weights_of(w_ref, distance, w_ref.shape[2] // 2), low, out_ref.at[:, at])
 
 
 def kernel_cost(depth, shape, chunks):
@@ -105,46 +107,42 @@
     )
 
 
-def first_partials(distances, rest, stack, flat):
+def first_partials(distances, stack, flat):
     count, owned, pixels = stack.shape
-    depth = flat.shape[0]
+    depth, width = flat.shape[0], 4 * owned
+    blocks = flat.shape[1] // width
     vmem, hbm = pl.BlockSpec(memory_space=pltpu.VMEM), pl.BlockSpec(memory_space=pltpu.HBM)
     return pl.pallas_call(
-        functools.partial(first_kernel, distances, rest),
+        functools.partial(first_kernel, distances),
         in_specs=[hbm, hbm],
         out_specs=[vmem] * 3,
         out_shape=[
             jax.ShapeDtypeStruct((depth, count * pixels), jnp.bfloat16),
             jax.ShapeDtypeStruct((2, len(distances), *stack.shape), jnp.float32),
-            jax.ShapeDtypeStruct((len(rest), depth, 2 * owned), jnp.bfloat16),
+            jax.ShapeDtypeStruct((blocks, depth, width), jnp.bfloat16),
         ],
-        scratch_shapes=[
-            pltpu.VMEM(stack.shape, jnp.bfloat16),
-            pltpu.VMEM((len(distances), depth, 2 * owned), jnp.bfloat16),
-            pltpu.SemaphoreType.DMA((1 + len(distances) + len(rest),)),
-        ],
+        scratch_shapes=[pltpu.VMEM(stack.shape, jnp.bfloat16), pltpu.SemaphoreType.DMA((blocks + 1,))],
         compiler_params=pltpu.CompilerParams(vmem_limit_bytes=24 * 2**20),
         cost_estimate=kernel_cost(depth, stack.shape, len(distances)),
         name="partials_and_patches",
     )(pltpu.with_memory_space_constraint(stack, pltpu.HBM), pltpu.with_memory_space_constraint(flat, pltpu.HBM))
 
 
-def next_partials(patches, weights, first, chunks, shape, before):
+def next_partials(distances, patches, weights, shape, before):
     vmem, unread = pl.BlockSpec(memory_space=pltpu.VMEM), pl.BlockSpec(memory_space=pl.ANY)
     return pl.pallas_call(
-        functools.partial(next_kernel, first),
+        functools.partial(next_kernel, distances),
         in_specs=[vmem, vmem] + [unread] * len(before),
         out_specs=vmem,
-        out_shape=jax.ShapeDtypeStruct((2, chunks, *shape), jnp.float32),
+        out_shape=jax.ShapeDtypeStruct((2, len(distances), *shape), jnp.float32),
         compiler_params=pltpu.CompilerParams(vmem_limit_bytes=24 * 2**20),
-        cost_estimate=kernel_cost(patches.shape[0], shape, chunks),
-        name="partials_" + str(first),
+        cost_estimate=kernel_cost(patches.shape[0], shape, len(distances)),
+        name="partials_" + "_".join(map(str, distances)),
     )(patches, weights, *before)
 
 
 def conv_halving(stack, flat, layer_bias):
     shape = stack.shape
-    images = range(shape[0])
     size = lax.axis_size(AXIS)
 
     def swap(value, bits):
@@ -159,40 +157,33 @@
             first = distances.index(part[0])
             came = swap(out[1, first : first + len(part)].astype(SENT), 1)
             for k, d in enumerate(part):
-                sums[d] = [out[0, first + k, i] + wide(came[k, i]) for i in images]
+                sums[d] = out[0, first + k] + wide(came[k])
         return sums
 
     def across(sums, bit):
-        came = swap(jnp.stack([value.astype(SENT) for value in sums]), 2 * bit)
-        return [wide(came[i]) for i in images]
-
-    def plus(sums, *others):
-        for other in others:
-            sums = [a + b for a, b in zip(sums, other)]
-        return sums
+        return wide(swap(sums.astype(SENT), 2 * bit))
 
     odd, even, near = (7, 5), (6, 4), (3, 1, 2, 0)
-    patches, odd_out, weights = first_partials(odd, even + near, stack, flat)
-    even_out = next_partials(patches, weights, 0, len(even), shape, (odd_out,))
+    patches, odd_out, weights = first_partials(odd, stack, flat)
+    even_out = next_partials(even, patches, weights, shape, (odd_out,))
     sums = core_sums(odd, (odd,), odd_out)
     sums.update(core_sums(even, (even,), even_out))
-    near_out = next_partials(patches, weights, len(even), len(near), shape, (even_out, sums[7][0]))
+    near_out = next_partials(near, patches, weights, shape, (even_out, sums[7]))
     sums.update(core_sums(near, ((3,), (1, 2), (0,)), near_out))
     came5 = across(sums[5], 1)
-    came6 = across(plus(sums[6], across(sums[7], 1)), 2)
-    came4 = across(plus(sums[4], came5, came6), 4)
-    came2 = across(plus(sums[2], across(sums[3], 1)), 2)
+    came6 = across(sums[6] + across(sums[7], 1), 2)
+    came4 = across(sums[4] + came5 + came6, 4)
+    came2 = across(sums[2] + across(sums[3], 1), 2)
     came1 = across(sums[1], 1)
-    total = plus(sums[0], came4, came2, came1)
-    bias = layer_bias[:, None]
-    return jnp.stack([(wide(stack[i]) + jnp.maximum(total[i] + bias, 0.0)).astype(jnp.bfloat16) for i in images])
+    total = sums[0] + came4 + came2 + came1
+    return (wide(stack) + jnp.maximum(total + layer_bias[:, None], 0.0)).astype(jnp.bfloat16)
 
 
 def local(size, maps, kernels, bias):
     for layer in range(kernels.shape[0]):
         owned = maps.shape[1]
         flat = kernels[layer].reshape(9 * owned, kernels.shape[3])
-        if size == 16 and owned % 64 == 0 and maps.shape[2] % 128 == 0:
+        if size == 16 and owned % 64 == 0 and maps.shape[2] % 128 == 0 and kernels.shape[3] == size * owned:
             maps = conv_halving(maps, flat, bias[layer])
         else:
             maps = conv_plain(maps, flat, bias[layer])

time: 34.2 us -> 33.8 us (0.988)
  other arithmetic: 2.09 us -> 1.73 us
    another operation x9 -> x1, other arithmetic: 1.31 us -> 0.27 us  [the longest x1 0.7 us: conv_halving(): jnp.stack([(wide(stack[i]) + jnp.maximum(total[i] + bias, 0.0)).astype(jn...]
    convert_element_type x6, other arithmetic: 0.63 us -> 1.34 us  [the longest x1 0.87 us: conv_halving(): (wide(stack) + jnp.maximum(total + layer_bias[:, None], 0.0)).astype(jnp....]
  transfers between devices with their start and end apart: 12 -> 12, of which waited for: 4 -> 4; matrix products, arithmetic and copies ran while one was open for 4% -> 3% of each run, Pallas kernels for 14% -> 14%
where the time goes in v5:
time: 33.8 us; the launch traced here: 33.7 us
  starting transfers between devices  14.2 us (42%)
  Pallas kernels  8.96 us (27%)
  waiting for transfers between devices  8.49 us (25%)
  other arithmetic  1.73 us (5%)
    ppermute x12, starting transfers between devices, swap(): return lax.ppermute(value, AXIS, [(i, i ^ bits) for i in range(size)])  14.2 us
    ppermute x12, waiting for transfers between devices, swap(): return lax.ppermute(value, AXIS, [(i, i ^ bits) for i in range(size)])  8.49 us
    pallas_call x2, Pallas kernels, next_partials(): pl.pallas_call(functools.partial(next_kernel, distances), in_specs=[vmem,...  4.68 us
    pallas_call x1, Pallas kernels, first_partials(): pl.pallas_call(functools.partial(first_kernel, distances), in_specs=[hbm,...  4.29 us
    convert_element_type x1, other arithmetic, conv_halving(): (wide(stack) + jnp.maximum(total + layer_bias[:, None], 0.0)).astype(jnp....  0.87 us
  transfers between devices with their start and end apart: 12, of which 4 were waited for; matrix products, arithmetic and copies ran while one was open for 3% of the time, Pallas kernels for 14%

profile of v5, /device:TPU:0, one launch (start us, length us, event | category | flops | bytes accessed | tf_op | source)
XLA Modules:
  0.0 33.7 jit_solution(15649068068955225703)
XLA Ops:
  0.0 4.3 %partials_and_patches.1 = (bf16[1728,512]{1,0:T(8,128)(2,1)S(1)}, f32[2,2,2,192,256]{4,3,2,1,0:T(8,128)S(1)}, bf16[4,1728,768]{2,1,0:T(8,128)(2,1)S(1)}) custom-call(bf16[2,192,256]{2,1,0:T(8,128)(2,1)} %maps_ref.1, bf16[1728,3072]{1,0:T(8,128)(2,1)} %bitcast.110), custom_call_target="tpu_custom_call" | custom-call | flops 1358954496 | bytes 2654208 | tf_op jit(solution)/shard_map/partials_and_patches/pallas_call | solution.py:115
  4.4 0.5 %collective-permute-start = (f16[2,2,192,256]{3,2,1,0:T(8,128)(2,1)S(1)}, f16[2,2,192,256]{3,2,1,0:T(8,128)(2,1)S(1)}, u32[]{:S(2)}, u32[]{:S(2)}) collective-permute-start(f16[2,2,192,256]{3,2,1,0:T(8,128)(2,1)S(1)} %fusion), channel_id=1, source_target_pairs={{0,1},{1,0},{2,3},{3,2},{4,5},{5,4},{6,7},{7,6},{8,9},{9,8},{10,11... | collective-permute-start | bytes 1179656 | tf_op jit(solution)/shard_map/ppermute | solution.py:149
  4.9 1.6 %partials_6_4.1.refs_0_ = f32[2,2,2,192,256]{4,3,2,1,0:T(8,128)S(1)} custom-call(bf16[1728,512]{1,0:T(8,128)(2,1)S(1)} %get-tuple-element.8.x_ref, bf16[4,1728,768]{2,1,0:T(8,128)(2,1)S(1)} %get-tuple-element.9.w_ref, f32[2,2,2,192,256]{4,3,2,1,0:T(8,128)S(1)} %get-tuple-element.10.refs_0_), custom_call_target="tpu_custom_call" | custom-call | flops 1358954496 | bytes 2654208 | tf_op jit(solution)/shard_map/partials_6_4/pallas_call | solution.py:133
  6.6 0.1 collective-permute-start.2
  6.7 0.1 fusion.25
  6.8 3.0 %collective-permute-start.4 = (f16[2,192,256]{2,1,0:T(8,128)(2,1)S(1)}, f16[2,192,256]{2,1,0:T(8,128)(2,1)S(1)}, u32[]{:S(2)}, u32[]{:S(2)}) collective-permute-start(f16[2,192,256]{2,1,0:T(8,128)(2,1)S(1)} %get-tuple-element.11), channel_id=1, source_target_pairs={{0,2},{1,3},{2,0},{3,1},{4,6},{5,7},{6,4},{7,5},{8,10},{9,11},{10,... | collective-permute-start | bytes 589832 | tf_op jit(solution)/shard_map/ppermute | solution.py:149
  9.9 3.1 %partials_3_1_2_0.1 = f32[2,4,2,192,256]{4,3,2,1,0:T(8,128)S(1)} custom-call(bf16[1728,512]{1,0:T(8,128)(2,1)S(1)} %get-tuple-element.8.x_ref, bf16[4,1728,768]{2,1,0:T(8,128)(2,1)S(1)} %get-tuple-element.9.w_ref, f32[2,2,2,192,256]{4,3,2,1,0:T(8,128)S(1)} %partials_6_4.1.refs_0_, f32[2,192,256]{2,1,0:T(8,128)S(1)} %get-tuple-element.12.refs_1_), custom_call_target="tpu_custom_call" | custom-call | flops 2717908992 | bytes 5308416 | tf_op jit(solution)/shard_map/partials_3_1_2_0/pallas_call | solution.py:133
  13.0 0.3 convert.20
  13.3 0.1 slice_bitcast_fusion.13
  13.4 0.1 slice_bitcast_fusion.2
  13.5 0.6 %collective-permute-start.7 = (f16[2,2,192,256]{3,2,1,0:T(8,128)(2,1)S(1)}, f16[2,2,192,256]{3,2,1,0:T(8,128)(2,1)S(1)}, u32[]{:S(2)}, u32[]{:S(2)}) collective-permute-start(f16[2,2,192,256]{3,2,1,0:T(8,128)(2,1)S(1)} %slice_bitcast_fusion.2), channel_id=1, source_target_pairs={{0,1},{1,0},{2,3},{3,2},{4,5},{5,4},{6,7},{7,6},{8,9},{9,8},{10,11... | collective-permute-start | bytes 1179656 | tf_op jit(solution)/shard_map/ppermute | solution.py:149
  14.1 0.1 collective-permute-start.1
  14.2 1.4 %collective-permute-done.4 = f16[2,192,256]{2,1,0:T(8,128)(2,1)S(1)} collective-permute-done((f16[2,192,256]{2,1,0:T(8,128)(2,1)S(1)}, f16[2,192,256]{2,1,0:T(8,128)(2,1)S(1)}, u32[]{:S(2)}, u32[]{:S(2)}) %collective-permute-start.4) | collective-permute-done | bytes 196640 | tf_op jit(solution)/shard_map/ppermute | solution.py:149
  15.6 2.2 %collective-permute-start.5 = (f16[2,192,256]{2,1,0:T(8,128)(2,1)S(1)}, f16[2,192,256]{2,1,0:T(8,128)(2,1)S(1)}, u32[]{:S(2)}, u32[]{:S(2)}) collective-permute-start(f16[2,192,256]{2,1,0:T(8,128)(2,1)S(1)} %fusion.11), channel_id=1, source_target_pairs={{0,4},{1,5},{2,6},{3,7},{4,0},{5,1},{6,2},{7,3},{8,12},{9,13},{10,... | collective-permute-start | bytes 589832 | tf_op jit(solution)/shard_map/ppermute | solution.py:149
  17.9 1.6 %collective-permute-start.9 = (f16[2,192,256]{2,1,0:T(8,128)(2,1)S(1)}, f16[2,192,256]{2,1,0:T(8,128)(2,1)S(1)}, u32[]{:S(2)}, u32[]{:S(2)}) collective-permute-start(f16[2,192,256]{2,1,0:T(8,128)(2,1)S(1)} %fusion.5), channel_id=1, source_target_pairs={{0,2},{1,3},{2,0},{3,1},{4,6},{5,7},{6,4},{7,5},{8,10},{9,11},{10,... | collective-permute-start | bytes 589832 | tf_op jit(solution)/shard_map/ppermute | solution.py:149
  19.5 2.3 %collective-permute-done.5 = f16[2,192,256]{2,1,0:T(8,128)(2,1)S(1)} collective-permute-done((f16[2,192,256]{2,1,0:T(8,128)(2,1)S(1)}, f16[2,192,256]{2,1,0:T(8,128)(2,1)S(1)}, u32[]{:S(2)}, u32[]{:S(2)}) %collective-permute-start.5) | collective-permute-done | bytes 196640 | tf_op jit(solution)/shard_map/ppermute | solution.py:149
  21.8 0.1 fusion.15
  21.9 2.8 %collective-permute-start.6 = (f16[2,192,256]{2,1,0:T(8,128)(2,1)S(1)}, f16[2,192,256]{2,1,0:T(8,128)(2,1)S(1)}, u32[]{:S(2)}, u32[]{:S(2)}) collective-permute-start(f16[2,192,256]{2,1,0:T(8,128)(2,1)S(1)} %fusion.15), channel_id=1, source_target_pairs={{0,8},{1,9},{2,10},{3,11},{4,12},{5,13},{6,14},{7,15},{8,0},{9,1},... | collective-permute-start | bytes 589832 | tf_op jit(solution)/shard_map/ppermute | solution.py:149
  24.7 0.1 fusion.8
  24.9 1.6 %collective-permute-start.10 = (f16[2,192,256]{2,1,0:T(8,128)(2,1)S(1)}, f16[2,192,256]{2,1,0:T(8,128)(2,1)S(1)}, u32[]{:S(2)}, u32[]{:S(2)}) collective-permute-start(f16[2,192,256]{2,1,0:T(8,128)(2,1)S(1)} %get-tuple-element.13), channel_id=1, source_target_pairs={{0,4},{1,5},{2,6},{3,7},{4,0},{5,1},{6,2},{7,3},{8,12},{9,13},{10,... | collective-permute-start | bytes 589832 | tf_op jit(solution)/shard_map/ppermute | solution.py:149
  26.5 1.5 %collective-permute-start.11 = (f16[2,192,256]{2,1,0:T(8,128)(2,1)S(1)}, f16[2,192,256]{2,1,0:T(8,128)(2,1)S(1)}, u32[]{:S(2)}, u32[]{:S(2)}) collective-permute-start(f16[2,192,256]{2,1,0:T(8,128)(2,1)S(1)} %get-tuple-element.14), channel_id=1, source_target_pairs={{0,2},{1,3},{2,0},{3,1},{4,6},{5,7},{6,4},{7,5},{8,10},{9,11},{10,... | collective-permute-start | bytes 589832 | tf_op jit(solution)/shard_map/ppermute | solution.py:149
  28.0 4.2 %collective-permute-done.6 = f16[2,192,256]{2,1,0:T(8,128)(2,1)S(1)} collective-permute-done((f16[2,192,256]{2,1,0:T(8,128)(2,1)S(1)}, f16[2,192,256]{2,1,0:T(8,128)(2,1)S(1)}, u32[]{:S(2)}, u32[]{:S(2)}) %collective-permute-start.6) | collective-permute-done | bytes 196640 | tf_op jit(solution)/shard_map/ppermute | solution.py:149
  32.2 0.6 %collective-permute-done.10 = f16[2,192,256]{2,1,0:T(8,128)(2,1)S(1)} collective-permute-done((f16[2,192,256]{2,1,0:T(8,128)(2,1)S(1)}, f16[2,192,256]{2,1,0:T(8,128)(2,1)S(1)}, u32[]{:S(2)}, u32[]{:S(2)}) %collective-permute-start.10) | collective-permute-done | bytes 196640 | tf_op jit(solution)/shard_map/ppermute | solution.py:149
  32.8 0.9 %fusion.23 = bf16[2,192,256]{2,1,0:T(8,128)(2,1)} fusion(f32[2,4,2,192,256]{4,3,2,1,0:T(8,128)S(1)} %partials_3_1_2_0.1, f16[2,192,256]{2,1,0:T(8,128)(2,1)S(1)} %collective-permute-done.11, f16[2,192,256]{2,1,0:T(8,128)(2,1)S(1)} %collective-permute-done.10, f16[2,192,256]{2,1,0:T(8,128)(2,1)S(1)} %collective-permute-done.6, ...), kind=kLoop, calls=%fused_computation.32 | loop fusion | flops 1277952 | bytes 1573632 | tf_op jit(solution)/shard_map/convert_element_type | solution.py:179
  (18 shorter events, 0.4 us)
Async XLA Ops:
  4.4 2.3 %collective-permute-start = (f16[2,2,192,256]{3,2,1,0:T(8,128)(2,1)S(1)}, f16[2,2,192,256]{3,2,1,0:T(8,128)(2,1)S(1)}, u32[]{:S(2)}, u32[]{:S(2)}) collective-permute-start(f16[2,2,192,256]{3,2,1,0:T(8,128)(2,1)S(1)} %fusion), channel_id=1, source_target_pairs={{0,1},{1,0},{2,3},{3,2},{4,5},{5,4},{6,7},{7,6},{8,9},{9,8},{10,11... | collective-permute-start | bytes 1179656 | tf_op jit(solution)/shard_map/ppermute | solution.py:149
  6.6 7.5 %collective-permute-start.2 = (f16[2,2,192,256]{3,2,1,0:T(8,128)(2,1)S(1)}, f16[2,2,192,256]{3,2,1,0:T(8,128)(2,1)S(1)}, u32[]{:S(2)}, u32[]{:S(2)}) collective-permute-start(f16[2,2,192,256]{3,2,1,0:T(8,128)(2,1)S(1)} %fusion.1), channel_id=1, source_target_pairs={{0,1},{1,0},{2,3},{3,2},{4,5},{5,4},{6,7},{7,6},{8,9},{9,8},{10,11... | collective-permute-start | bytes 1179656 | tf_op jit(solution)/shard_map/ppermute | solution.py:149
  6.8 8.7 %collective-permute-start.4 = (f16[2,192,256]{2,1,0:T(8,128)(2,1)S(1)}, f16[2,192,256]{2,1,0:T(8,128)(2,1)S(1)}, u32[]{:S(2)}, u32[]{:S(2)}) collective-permute-start(f16[2,192,256]{2,1,0:T(8,128)(2,1)S(1)} %get-tuple-element.11), channel_id=1, source_target_pairs={{0,2},{1,3},{2,0},{3,1},{4,6},{5,7},{6,4},{7,5},{8,10},{9,11},{10,... | collective-permute-start | bytes 589832 | tf_op jit(solution)/shard_map/ppermute | solution.py:149
  9.9 9.6 %collective-permute-start.3 = (f16[2,192,256]{2,1,0:T(8,128)(2,1)S(1)}, f16[2,192,256]{2,1,0:T(8,128)(2,1)S(1)}, u32[]{:S(2)}, u32[]{:S(2)}) collective-permute-start(f16[2,192,256]{2,1,0:T(8,128)(2,1)S(1)} %get-tuple-element.15), channel_id=1, source_target_pairs={{0,2},{1,3},{2,0},{3,1},{4,6},{5,7},{6,4},{7,5},{8,10},{9,11},{10,... | collective-permute-start | bytes 589832 | tf_op jit(solution)/shard_map/ppermute | solution.py:149
  13.4 4.5 %collective-permute-start.8 = (f16[1,2,192,256]{3,2,1,0:T(8,128)(2,1)S(1)}, f16[1,2,192,256]{3,2,1,0:T(8,128)(2,1)S(1)}, u32[]{:S(2)}, u32[]{:S(2)}) collective-permute-start(f16[1,2,192,256]{3,2,1,0:T(8,128)(2,1)S(1)} %get-tuple-element.17), channel_id=1, source_target_pairs={{0,1},{1,0},{2,3},{3,2},{4,5},{5,4},{6,7},{7,6},{8,9},{9,8},{10,11... | collective-permute-start | bytes 589832 | tf_op jit(solution)/shard_map/ppermute | solution.py:149
  13.5 11.2 %collective-permute-start.7 = (f16[2,2,192,256]{3,2,1,0:T(8,128)(2,1)S(1)}, f16[2,2,192,256]{3,2,1,0:T(8,128)(2,1)S(1)}, u32[]{:S(2)}, u32[]{:S(2)}) collective-permute-start(f16[2,2,192,256]{3,2,1,0:T(8,128)(2,1)S(1)} %slice_bitcast_fusion.2), channel_id=1, source_target_pairs={{0,1},{1,0},{2,3},{3,2},{4,5},{5,4},{6,7},{7,6},{8,9},{9,8},{10,11... | collective-permute-start | bytes 1179656 | tf_op jit(solution)/shard_map/ppermute | solution.py:149
  14.1 14.0 %collective-permute-start.1 = (f16[1,2,192,256]{3,2,1,0:T(8,128)(2,1)S(1)}, f16[1,2,192,256]{3,2,1,0:T(8,128)(2,1)S(1)}, u32[]{:S(2)}, u32[]{:S(2)}) collective-permute-start(f16[1,2,192,256]{3,2,1,0:T(8,128)(2,1)S(1)} %get-tuple-element.16), channel_id=1, source_target_pairs={{0,1},{1,0},{2,3},{3,2},{4,5},{5,4},{6,7},{7,6},{8,9},{9,8},{10,11... | collective-permute-start | bytes 589832 | tf_op jit(solution)/shard_map/ppermute | solution.py:149
  15.6 6.2 %collective-permute-start.5 = (f16[2,192,256]{2,1,0:T(8,128)(2,1)S(1)}, f16[2,192,256]{2,1,0:T(8,128)(2,1)S(1)}, u32[]{:S(2)}, u32[]{:S(2)}) collective-permute-start(f16[2,192,256]{2,1,0:T(8,128)(2,1)S(1)} %fusion.11), channel_id=1, source_target_pairs={{0,4},{1,5},{2,6},{3,7},{4,0},{5,1},{6,2},{7,3},{8,12},{9,13},{10,... | collective-permute-start | bytes 589832 | tf_op jit(solution)/shard_map/ppermute | solution.py:149
  17.9 14.9 %copy-start = (bf16[2,192,256]{2,1,0:T(8,128)(2,1)S(1)}, bf16[2,192,256]{2,1,0:T(8,128)(2,1)}, u32[]{:S(2)}) copy-start(bf16[2,192,256]{2,1,0:T(8,128)(2,1)} %maps_ref.1) | copy-start | bytes 589828
  17.9 14.9 %copy-start.1 = (f32[1,192]{1,0:T(1,128)S(1)}, f32[1,192]{1,0:T(1,128)}, u32[]{:S(2)}) copy-start(f32[1,192]{1,0:T(1,128)} %param.5) | copy-start | bytes 2308
  17.9 6.8 %collective-permute-start.9 = (f16[2,192,256]{2,1,0:T(8,128)(2,1)S(1)}, f16[2,192,256]{2,1,0:T(8,128)(2,1)S(1)}, u32[]{:S(2)}, u32[]{:S(2)}) collective-permute-start(f16[2,192,256]{2,1,0:T(8,128)(2,1)S(1)} %fusion.5), channel_id=1, source_target_pairs={{0,2},{1,3},{2,0},{3,1},{4,6},{5,7},{6,4},{7,5},{8,10},{9,11},{10,... | collective-permute-start | bytes 589832 | tf_op jit(solution)/shard_map/ppermute | solution.py:149
  21.9 10.3 %collective-permute-start.6 = (f16[2,192,256]{2,1,0:T(8,128)(2,1)S(1)}, f16[2,192,256]{2,1,0:T(8,128)(2,1)S(1)}, u32[]{:S(2)}, u32[]{:S(2)}) collective-permute-start(f16[2,192,256]{2,1,0:T(8,128)(2,1)S(1)} %fusion.15), channel_id=1, source_target_pairs={{0,8},{1,9},{2,10},{3,11},{4,12},{5,13},{6,14},{7,15},{8,0},{9,1},... | collective-permute-start | bytes 589832 | tf_op jit(solution)/shard_map/ppermute | solution.py:149
  24.9 7.9 %collective-permute-start.10 = (f16[2,192,256]{2,1,0:T(8,128)(2,1)S(1)}, f16[2,192,256]{2,1,0:T(8,128)(2,1)S(1)}, u32[]{:S(2)}, u32[]{:S(2)}) collective-permute-start(f16[2,192,256]{2,1,0:T(8,128)(2,1)S(1)} %get-tuple-element.13), channel_id=1, source_target_pairs={{0,4},{1,5},{2,6},{3,7},{4,0},{5,1},{6,2},{7,3},{8,12},{9,13},{10,... | collective-permute-start | bytes 589832 | tf_op jit(solution)/shard_map/ppermute | solution.py:149
  26.5 6.3 %collective-permute-start.11 = (f16[2,192,256]{2,1,0:T(8,128)(2,1)S(1)}, f16[2,192,256]{2,1,0:T(8,128)(2,1)S(1)}, u32[]{:S(2)}, u32[]{:S(2)}) collective-permute-start(f16[2,192,256]{2,1,0:T(8,128)(2,1)S(1)} %get-tuple-element.14), channel_id=1, source_target_pairs={{0,2},{1,3},{2,0},{3,1},{4,6},{5,7},{6,4},{7,5},{8,10},{9,11},{10,... | collective-permute-start | bytes 589832 | tf_op jit(solution)/shard_map/ppermute | solution.py:149
